TPU v7x, 32 devices: a whole 2x2x4 slice. The times are simulated.
32 devices in a mesh: dp: 8 (over z, x), rep: 4 (over y, core).
Axes of the slice: x: 2, y: 2, z: 4, core: 2. Of those that a mesh axis runs over, the one named last changes fastest.
Arguments:
- input_160: bfloat16 [128, 10, 10, 1024], P(('dp', 'rep')), may hold values from -6 to 6
- input_224: bfloat16 [64, 14, 14, 1024], P(('dp', 'rep')), may hold values from -6 to 6
- input_288: bfloat16 [64, 18, 18, 1024], P(('dp', 'rep')), may hold values from -6 to 6
- cotangent_160: bfloat16 [128, 5, 5, 2048], P(('dp', 'rep')), may hold values from -6 to 6
- cotangent_224: bfloat16 [64, 7, 7, 2048], P(('dp', 'rep')), may hold values from -6 to 6
- cotangent_288: bfloat16 [64, 9, 9, 2048], P(('dp', 'rep')), may hold values from -6 to 6
- live_counts: int32 [32, 3], P(('dp', 'rep')), may hold values from 1 to 4, as said below
- conv_a1: bfloat16 [1024, 512], P(None, 'dp'), may hold values from -0.1875 to 0.1875
- norm_a1: bfloat16 [2, 512], P(None, 'dp')
- conv_a2: bfloat16 [3, 3, 512, 512], P(None, None, None, 'dp'), may hold values from -0.09375 to 0.09375
- norm_a2: bfloat16 [2, 512], P(None, 'dp')
- conv_a3: bfloat16 [512, 2048], P(None, 'dp'), may hold values from -0.25 to 0.25
- norm_a3: bfloat16 [2, 2048], P(None, 'dp')
- conv_as: bfloat16 [1024, 2048], P(None, 'dp'), may hold values from -0.1875 to 0.1875
- norm_as: bfloat16 [2, 2048], P(None, 'dp')
- conv_b1: bfloat16 [2048, 512], P(None, 'dp'), may hold values from -0.125 to 0.125
- norm_b1: bfloat16 [2, 512], P(None, 'dp')
- conv_b2: bfloat16 [3, 3, 512, 512], P(None, None, None, 'dp'), may hold values from -0.09375 to 0.09375
- norm_b2: bfloat16 [2, 512], P(None, 'dp')
- conv_b3: bfloat16 [512, 2048], P(None, 'dp'), may hold values from -0.25 to 0.25
- norm_b3: bfloat16 [2, 2048], P(None, 'dp')
Outputs:
- output_160: bfloat16 [128, 5, 5, 2048], P(('dp', 'rep'))
- output_224: bfloat16 [64, 7, 7, 2048], P(('dp', 'rep'))
- output_288: bfloat16 [64, 9, 9, 2048], P(('dp', 'rep'))
- grad_input_160: bfloat16 [128, 10, 10, 1024], P(('dp', 'rep'))
- grad_input_224: bfloat16 [64, 14, 14, 1024], P(('dp', 'rep'))
- grad_input_288: bfloat16 [64, 18, 18, 1024], P(('dp', 'rep'))
- grad_conv_a1: float32 [1024, 512], P(None, 'dp')
- grad_norm_a1: float32 [2, 512], P(None, 'dp')
- grad_conv_a2: float32 [3, 3, 512, 512], P(None, None, None, 'dp')
- grad_norm_a2: float32 [2, 512], P(None, 'dp')
- grad_conv_a3: float32 [512, 2048], P(None, 'dp')
- grad_norm_a3: float32 [2, 2048], P(None, 'dp')
- grad_conv_as: float32 [1024, 2048], P(None, 'dp')
- grad_norm_as: float32 [2, 2048], P(None, 'dp')
- grad_conv_b1: float32 [2048, 512], P(None, 'dp')
- grad_norm_b1: float32 [2, 512], P(None, 'dp')
- grad_conv_b2: float32 [3, 3, 512, 512], P(None, None, None, 'dp')
- grad_norm_b2: float32 [2, 512], P(None, 'dp')
- grad_conv_b3: float32 [512, 2048], P(None, 'dp')
- grad_norm_b3: float32 [2, 2048], P(None, 'dp')
- lars_conv_a1: float32 [1024, 512], P(None, 'dp')
- lars_conv_a2: float32 [3, 3, 512, 512], P(None, None, None, 'dp')
- lars_conv_a3: float32 [512, 2048], P(None, 'dp')
- lars_conv_as: float32 [1024, 2048], P(None, 'dp')
- lars_conv_b1: float32 [2048, 512], P(None, 'dp')
- lars_conv_b2: float32 [3, 3, 512, 512], P(None, None, None, 'dp')
- lars_conv_b3: float32 [512, 2048], P(None, 'dp')
- norm_sums: float32 [2, 7], replicated
Inputs may be any that keep to these rules, and one draw needn't show every extreme that they name: `live_counts`: column k of a device is at least 1 and at most that group's slots on one device (4, 2, 2); in each column some device is full and some holds one image.
All inputs are finite; a program needn't handle non-finite values.
Results may differ from a plain program's by a relative error of at most 0.019.
Values may be sent and summed in bfloat16 or wider, within the bound.
A program may use at most 144 MiB of HBM per device.

v0:
```python
import functools

import jax
import jax.numpy as jnp
import numpy as np
from jax import lax
from jax.experimental import pallas as pl
from jax.experimental.pallas import tpu as pltpu
from jax.sharding import PartitionSpec as P

DP, REP = "dp", "rep"
EPSILON = 1e-05
DECAY_RATE = 5e-05


def silu_slope(values):
    sigmoid = jax.nn.sigmoid(values)
    return sigmoid * (1.0 + values * (1.0 - sigmoid))


def pointwise(inputs, weight):
    return jnp.tensordot(inputs, weight, 1, preferred_element_type=jnp.float32)


def pointwise_back(upstream, weight):
    return jnp.tensordot(upstream, weight, ((3,), (1,)), preferred_element_type=jnp.float32)


def weight_term(inputs, upstream):
    return jnp.tensordot(inputs, upstream, ((0, 1, 2),) * 2, preferred_element_type=jnp.float32)


def summed_terms(inputs, upstream):
    running = weight_term(inputs[0], upstream[0])
    for group_member in (1, 2):
        running = running + weight_term(inputs[group_member], upstream[group_member])
    return running


def patches(inputs, stride):
    padded = jnp.pad(inputs, ((0, 0), (1, 1), (1, 1), (0, 0)))
    extent = inputs.shape[1]
    pieces = []
    for offset_row in range(3):
        for offset_col in range(3):
            pieces.append(
                padded[
                    :,
                    offset_row : offset_row + extent : stride,
                    offset_col : offset_col + extent : stride,
                    :,
                ]
            )
    return jnp.concatenate(pieces, axis=3)


def fold_patches(upstream, stride, side_in):
    channels = upstream.shape[3] // 9
    padded = jnp.zeros((upstream.shape[0], side_in + 2, side_in + 2, channels), jnp.float32)
    for offset_row in range(3):
        for offset_col in range(3):
            start_at = (offset_row * 3 + offset_col) * channels
            padded = padded.at[
                :,
                offset_row : offset_row + side_in : stride,
                offset_col : offset_col + side_in : stride,
                :,
            ].add(upstream[..., start_at : start_at + channels])
    return padded[:, 1 : side_in + 1, 1 : side_in + 1, :]


def batch_norm(values, live_masks, norm_param, totals):
    gain_row = norm_param[0].astype(jnp.float32)
    shift_row = norm_param[1].astype(jnp.float32)
    firsts = []
    seconds = []
    for group_member in range(3):
        weighted = values[group_member] * live_masks[group_member]
        firsts.append(jnp.sum(weighted, axis=(0, 1, 2)))
        seconds.append(jnp.sum(weighted * values[group_member], axis=(0, 1, 2)))
    summed = lax.psum(
        (firsts[0], seconds[0], firsts[1], seconds[1], firsts[2], seconds[2]), (DP, REP)
    )
    normed = []
    means = []
    scales = []
    for group_member in range(3):
        pixel_count = (
            totals[group_member] * values[group_member].shape[1] * values[group_member].shape[2]
        )
        mean_value = summed[2 * group_member] / pixel_count
        inv_std = lax.rsqrt(
            summed[2 * group_member + 1] / pixel_count - mean_value * mean_value + EPSILON
        )
        normed.append((values[group_member] - mean_value) * inv_std * gain_row + shift_row)
        means.append(mean_value)
        scales.append(inv_std)
    return (normed, means, scales)


def norm_back(upstream, values, live_masks, norm_param, means, scales, totals):
    gain_row = norm_param[0].astype(jnp.float32)
    normals = []
    firsts = []
    seconds = []
    for group_member in range(3):
        normal = (values[group_member] - means[group_member]) * scales[group_member]
        weighted = upstream[group_member] * live_masks[group_member]
        normals.append(normal)
        firsts.append(jnp.sum(weighted, axis=(0, 1, 2)))
        seconds.append(jnp.sum(weighted * normal, axis=(0, 1, 2)))
    summed = lax.psum(
        (firsts[0], seconds[0], firsts[1], seconds[1], firsts[2], seconds[2]), (DP, REP)
    )
    results = []
    for group_member in range(3):
        pixel_count = (
            totals[group_member] * values[group_member].shape[1] * values[group_member].shape[2]
        )
        centered = (
            upstream[group_member]
            - summed[2 * group_member] / pixel_count
            - normals[group_member] * (summed[2 * group_member + 1] / pixel_count)
        )
        results.append(
            (live_masks[group_member] * gain_row * scales[group_member] * centered).astype(
                jnp.bfloat16
            )
        )
    param_grad = jnp.stack([summed[1] + summed[3] + summed[5], summed[0] + summed[2] + summed[4]])
    return (results, param_grad)


def own_columns(full, local_width):
    return lax.dynamic_slice_in_dim(full, lax.axis_index(DP) * local_width, local_width, 1)


def plain_on_device(
    input_160,
    input_224,
    input_288,
    cotangent_160,
    cotangent_224,
    cotangent_288,
    live_counts,
    conv_a1,
    norm_a1,
    conv_a2,
    norm_a2,
    conv_a3,
    norm_a3,
    conv_as,
    norm_as,
    conv_b1,
    norm_b1,
    conv_b2,
    norm_b2,
    conv_b3,
    norm_b3,
):
    inputs = (input_160, input_224, input_288)
    cotangents = (cotangent_160, cotangent_224, cotangent_288)
    live_masks = []
    masked = []
    for group_member in range(3):
        group_slot_count = inputs[group_member].shape[0]
        live_flags = (
            (jnp.arange(group_slot_count) < live_counts[0, group_member])
            .astype(jnp.float32)
            .reshape(group_slot_count, 1, 1, 1)
        )
        live_masks.append(live_flags)
        masked.append(inputs[group_member] * live_flags.astype(jnp.bfloat16))
    totals = lax.psum(live_counts[0].astype(jnp.float32), (DP, REP))
    local_weights = (conv_a1, conv_a2, conv_a3, conv_as, conv_b1, conv_b2, conv_b3)
    squares_list = []
    for weight in local_weights:
        squares_list.append(jnp.sum(jnp.square(weight.astype(jnp.float32))))
    weight_squares = jnp.stack(squares_list)
    gathered_a = (
        lax.all_gather(conv_a1, DP, axis=1, tiled=True),
        lax.all_gather(norm_a1, DP, axis=1, tiled=True),
        lax.all_gather(conv_a2, DP, axis=3, tiled=True),
        lax.all_gather(norm_a2, DP, axis=1, tiled=True),
        lax.all_gather(conv_a3, DP, axis=1, tiled=True),
        lax.all_gather(norm_a3, DP, axis=1, tiled=True),
        lax.all_gather(conv_as, DP, axis=1, tiled=True),
        lax.all_gather(norm_as, DP, axis=1, tiled=True),
    )
    full_a1, param_a1, full_a2, param_a2, full_a3, param_a3, full_as, param_as = gathered_a
    mid_width = full_a2.shape[3]
    out_width = full_a3.shape[1]
    hidden_a1 = [pointwise(masked[group_member], full_a1) for group_member in range(3)]
    normed_a1, means_a1, scales_a1 = batch_norm(hidden_a1, live_masks, param_a1, totals)
    act_a1 = [
        jax.nn.silu(normed_a1[group_member]).astype(jnp.bfloat16) for group_member in range(3)
    ]
    kernel_a2 = full_a2.reshape(9 * mid_width, mid_width)
    hidden_a2 = [
        pointwise(patches(act_a1[group_member], 2), kernel_a2) for group_member in range(3)
    ]
    normed_a2, means_a2, scales_a2 = batch_norm(hidden_a2, live_masks, param_a2, totals)
    act_a2 = [
        jax.nn.silu(normed_a2[group_member]).astype(jnp.bfloat16) for group_member in range(3)
    ]
    strided = [masked[group_member][:, ::2, ::2, :] for group_member in range(3)]
    joined = [
        jnp.concatenate(
            [pointwise(act_a2[group_member], full_a3), pointwise(strided[group_member], full_as)],
            axis=3,
        )
        for group_member in range(3)
    ]
    param_joined = jnp.concatenate([param_a3, param_as], axis=1)
    normed_j, means_j, scales_j = batch_norm(joined, live_masks, param_joined, totals)
    sum_a = [
        normed_j[group_member][..., :out_width] + normed_j[group_member][..., out_width:]
        for group_member in range(3)
    ]
    out_a = [
        (jax.nn.silu(sum_a[group_member]) * live_masks[group_member]).astype(jnp.bfloat16)
        for group_member in range(3)
    ]
    gathered_b = (
        lax.all_gather(conv_b1, DP, axis=1, tiled=True),
        lax.all_gather(norm_b1, DP, axis=1, tiled=True),
        lax.all_gather(conv_b2, DP, axis=3, tiled=True),
        lax.all_gather(norm_b2, DP, axis=1, tiled=True),
        lax.all_gather(conv_b3, DP, axis=1, tiled=True),
        lax.all_gather(norm_b3, DP, axis=1, tiled=True),
    )
    full_b1, param_b1, full_b2, param_b2, full_b3, param_b3 = gathered_b
    hidden_b1 = [pointwise(out_a[group_member], full_b1) for group_member in range(3)]
    normed_b1, means_b1, scales_b1 = batch_norm(hidden_b1, live_masks, param_b1, totals)
    act_b1 = [
        jax.nn.silu(normed_b1[group_member]).astype(jnp.bfloat16) for group_member in range(3)
    ]
    kernel_b2 = full_b2.reshape(9 * mid_width, mid_width)
    hidden_b2 = [
        pointwise(patches(act_b1[group_member], 1), kernel_b2) for group_member in range(3)
    ]
    normed_b2, means_b2, scales_b2 = batch_norm(hidden_b2, live_masks, param_b2, totals)
    act_b2 = [
        jax.nn.silu(normed_b2[group_member]).astype(jnp.bfloat16) for group_member in range(3)
    ]
    hidden_b3 = [pointwise(act_b2[group_member], full_b3) for group_member in range(3)]
    normed_b3, means_b3, scales_b3 = batch_norm(hidden_b3, live_masks, param_b3, totals)
    sum_b = [
        normed_b3[group_member] + out_a[group_member].astype(jnp.float32)
        for group_member in range(3)
    ]
    outputs = [
        (jax.nn.silu(sum_b[group_member]) * live_masks[group_member]).astype(jnp.bfloat16)
        for group_member in range(3)
    ]
    back_b = (
        lax.all_gather(conv_b1, DP, axis=1, tiled=True),
        lax.all_gather(norm_b1, DP, axis=1, tiled=True),
        lax.all_gather(conv_b2, DP, axis=3, tiled=True),
        lax.all_gather(norm_b2, DP, axis=1, tiled=True),
        lax.all_gather(conv_b3, DP, axis=1, tiled=True),
        lax.all_gather(norm_b3, DP, axis=1, tiled=True),
    )
    full_b1, param_b1, full_b2, param_b2, full_b3, param_b3 = back_b
    kernel_b2 = full_b2.reshape(9 * mid_width, mid_width)
    grad_sum_b = [
        cotangents[group_member].astype(jnp.float32)
        * live_masks[group_member]
        * silu_slope(sum_b[group_member])
        for group_member in range(3)
    ]
    grad_h_b3, pgrad_b3 = norm_back(
        grad_sum_b, hidden_b3, live_masks, param_b3, means_b3, scales_b3, totals
    )
    term_b3 = summed_terms(act_b2, grad_h_b3)
    grad_act = [
        pointwise_back(grad_h_b3[group_member], full_b3) * silu_slope(normed_b2[group_member])
        for group_member in range(3)
    ]
    grad_h_b2, pgrad_b2 = norm_back(
        grad_act, hidden_b2, live_masks, param_b2, means_b2, scales_b2, totals
    )
    term_b2 = summed_terms(
        [patches(act_b1[group_member], 1) for group_member in range(3)], grad_h_b2
    ).reshape(3, 3, mid_width, mid_width)
    grad_act = [
        fold_patches(
            pointwise_back(grad_h_b2[group_member], kernel_b2), 1, act_b1[group_member].shape[1]
        )
        * silu_slope(normed_b1[group_member])
        for group_member in range(3)
    ]
    grad_h_b1, pgrad_b1 = norm_back(
        grad_act, hidden_b1, live_masks, param_b1, means_b1, scales_b1, totals
    )
    term_b1 = summed_terms(out_a, grad_h_b1)
    grad_out_a = [
        grad_sum_b[group_member] + pointwise_back(grad_h_b1[group_member], full_b1)
        for group_member in range(3)
    ]
    shard_b = (
        lax.psum_scatter(term_b1, DP, scatter_dimension=1, tiled=True),
        lax.psum_scatter(term_b2, DP, scatter_dimension=3, tiled=True),
        lax.psum_scatter(term_b3, DP, scatter_dimension=1, tiled=True),
    )
    grads_b = (
        lax.psum(shard_b[0].astype(jnp.bfloat16), REP).astype(jnp.float32),
        lax.psum(shard_b[1].astype(jnp.bfloat16), REP).astype(jnp.float32),
        lax.psum(shard_b[2].astype(jnp.bfloat16), REP).astype(jnp.float32),
    )
    back_a = (
        lax.all_gather(conv_a1, DP, axis=1, tiled=True),
        lax.all_gather(norm_a1, DP, axis=1, tiled=True),
        lax.all_gather(conv_a2, DP, axis=3, tiled=True),
        lax.all_gather(norm_a2, DP, axis=1, tiled=True),
        lax.all_gather(conv_a3, DP, axis=1, tiled=True),
        lax.all_gather(norm_a3, DP, axis=1, tiled=True),
        lax.all_gather(conv_as, DP, axis=1, tiled=True),
        lax.all_gather(norm_as, DP, axis=1, tiled=True),
    )
    full_a1, param_a1, full_a2, param_a2, full_a3, param_a3, full_as, param_as = back_a
    kernel_a2 = full_a2.reshape(9 * mid_width, mid_width)
    param_joined = jnp.concatenate([param_a3, param_as], axis=1)
    grad_sum_a = [
        grad_out_a[group_member] * live_masks[group_member] * silu_slope(sum_a[group_member])
        for group_member in range(3)
    ]
    grad_joined = [
        jnp.concatenate([grad_sum_a[group_member], grad_sum_a[group_member]], axis=3)
        for group_member in range(3)
    ]
    grad_h_j, pgrad_j = norm_back(
        grad_joined, joined, live_masks, param_joined, means_j, scales_j, totals
    )
    grad_h_a3 = [grad_h_j[group_member][..., :out_width] for group_member in range(3)]
    grad_h_as = [grad_h_j[group_member][..., out_width:] for group_member in range(3)]
    term_a3 = summed_terms(act_a2, grad_h_a3)
    term_as = summed_terms(strided, grad_h_as)
    grad_act = [
        pointwise_back(grad_h_a3[group_member], full_a3) * silu_slope(normed_a2[group_member])
        for group_member in range(3)
    ]
    grad_h_a2, pgrad_a2 = norm_back(
        grad_act, hidden_a2, live_masks, param_a2, means_a2, scales_a2, totals
    )
    term_a2 = summed_terms(
        [patches(act_a1[group_member], 2) for group_member in range(3)], grad_h_a2
    ).reshape(3, 3, mid_width, mid_width)
    grad_act = [
        fold_patches(
            pointwise_back(grad_h_a2[group_member], kernel_a2), 2, act_a1[group_member].shape[1]
        )
        * silu_slope(normed_a1[group_member])
        for group_member in range(3)
    ]
    grad_h_a1, pgrad_a1 = norm_back(
        grad_act, hidden_a1, live_masks, param_a1, means_a1, scales_a1, totals
    )
    term_a1 = summed_terms(masked, grad_h_a1)
    grad_inputs = [
        pointwise_back(grad_h_a1[group_member], full_a1)
        .at[:, ::2, ::2, :]
        .add(pointwise_back(grad_h_as[group_member], full_as))
        .astype(jnp.bfloat16)
        for group_member in range(3)
    ]
    shard_a = (
        lax.psum_scatter(term_a1, DP, scatter_dimension=1, tiled=True),
        lax.psum_scatter(term_a2, DP, scatter_dimension=3, tiled=True),
        lax.psum_scatter(term_a3, DP, scatter_dimension=1, tiled=True),
        lax.psum_scatter(term_as, DP, scatter_dimension=1, tiled=True),
    )
    grads_a = (
        lax.psum(shard_a[0].astype(jnp.bfloat16), REP).astype(jnp.float32),
        lax.psum(shard_a[1].astype(jnp.bfloat16), REP).astype(jnp.float32),
        lax.psum(shard_a[2].astype(jnp.bfloat16), REP).astype(jnp.float32),
        lax.psum(shard_a[3].astype(jnp.bfloat16), REP).astype(jnp.float32),
    )
    mid_local = norm_a1.shape[1]
    out_local = norm_a3.shape[1]
    norm_grad_a1 = own_columns(pgrad_a1, mid_local)
    norm_grad_a2 = own_columns(pgrad_a2, mid_local)
    norm_grad_a3 = own_columns(pgrad_j[:, :out_width], out_local)
    norm_grad_as = own_columns(pgrad_j[:, out_width:], out_local)
    norm_grad_b1 = own_columns(pgrad_b1, mid_local)
    norm_grad_b2 = own_columns(pgrad_b2, mid_local)
    norm_grad_b3 = own_columns(pgrad_b3, out_local)
    gradients = (grads_a[0], grads_a[1], grads_a[2], grads_a[3], grads_b[0], grads_b[1], grads_b[2])
    grad_list = []
    for gradient in gradients:
        grad_list.append(jnp.sum(gradient * gradient))
    grad_squares = jnp.stack(grad_list)
    weight_totals, grad_totals = lax.psum((weight_squares, grad_squares), DP)
    weight_norm = jnp.sqrt(weight_totals)
    grad_norm = jnp.sqrt(grad_totals)
    trust_ratio = weight_norm / (grad_norm + DECAY_RATE * weight_norm)
    scaled = [
        trust_ratio[layer_id]
        * (gradients[layer_id] + DECAY_RATE * local_weights[layer_id].astype(jnp.float32))
        for layer_id in range(7)
    ]
    return (
        outputs[0],
        outputs[1],
        outputs[2],
        grad_inputs[0],
        grad_inputs[1],
        grad_inputs[2],
        gradients[0],
        norm_grad_a1,
        gradients[1],
        norm_grad_a2,
        gradients[2],
        norm_grad_a3,
        gradients[3],
        norm_grad_as,
        gradients[4],
        norm_grad_b1,
        gradients[5],
        norm_grad_b2,
        gradients[6],
        norm_grad_b3,
        scaled[0],
        scaled[1],
        scaled[2],
        scaled[3],
        scaled[4],
        scaled[5],
        scaled[6],
        jnp.stack([weight_totals, grad_totals]),
    )


MESH = pl.DeviceIdType.MESH
ANY = pl.BlockSpec(memory_space=pl.ANY)


def position():
    dp, rep = lax.axis_index(DP), lax.axis_index(REP)
    return dp // 2, lax.rem(dp, 2), rep // 2, lax.rem(rep, 2)


def device_at(z, x, y, core):
    return (z * 2 + x, y * 2 + core)


def greet(depth, crosswise=False):
    z, x, y, core = position()
    barrier = pltpu.get_barrier_semaphore()
    peers = [(z, x, y, 1 - core), (z, x, 1 - y, core), (z, x, 1 - y, 1 - core)]
    peers += [(z, 1 - x, y, core), (z, 1 - x, y, 1 - core), (z, 1 - x, 1 - y, core), (z, 1 - x, 1 - y, 1 - core)]
    peers += [(lax.rem(z + step, depth), x, y, core) for step in range(1, depth)]
    if crosswise:
        peers += [(lax.rem(z + step, depth), 1 - x, y, core) for step in range(1, depth)]
    for peer in peers:
        pl.semaphore_signal(barrier, inc=1, device_id=device_at(*peer), device_id_type=MESH)
    pl.semaphore_wait(barrier, len(peers))


def remote(src, dst, send, recv, peer):
    return pltpu.make_async_remote_copy(
        src_ref=src, dst_ref=dst, send_sem=send, recv_sem=recv, device_id=device_at(*peer), device_id_type=MESH
    )


def chunk_rows(rows, both, y, core):
    if both:
        return pl.ds(pl.multiple_of(core * (rows // 2), rows // 2), rows // 2)
    return pl.ds(pl.multiple_of(core * (rows // 2) + y * (rows // 4), rows // 4), rows // 4)


def core_rows(rows, core):
    return pl.ds(pl.multiple_of(core * (rows // 2), rows // 2), rows // 2)


class Gather:
    AHEAD = 2

    def __init__(self, shards, fulls, sems, depth):
        self.shards, self.fulls, self.depth = shards, fulls, depth
        (self.local_sem, self.z_send, self.z_recv, self.x_send, self.x_recv) = sems[:5]
        (self.y_send, self.y_recv, self.c_send, self.c_recv) = sems[5:]
        self.z, self.x, self.y, self.core = position()
        self.count = len(GATHER_CHUNKS)
        self.z_next = self.x_next = self.y_next = self.c_next = 0

    @staticmethod
    def scratch(depth):
        dma, count = pltpu.SemaphoreType.DMA, len(GATHER_CHUNKS)
        return [dma((count,))] + [dma((count, depth - 1))] * 2 + [dma((count,))] * 6

    def part(self, k):
        tensor, lead, leads, both, column, columns = GATHER_CHUNKS[k]
        rows = chunk_rows(self.shards[tensor].shape[1], both, self.y, self.core)
        return self.fulls[tensor], pl.ds(lead, leads), rows, pl.ds(column, columns)

    def place(self, k):
        full, lead, rows, cols = self.part(k)
        shard = self.shards[GATHER_CHUNKS[k][0]]
        return pltpu.make_async_copy(
            shard.at[lead, rows, cols], full.at[self.z, self.x, lead, rows, cols], self.local_sem.at[k]
        )

    def z_copies(self, k):
        full, lead, rows, cols = self.part(k)
        here = full.at[self.z, self.x, lead, rows, cols]
        return [
            remote(
                here,
                here,
                self.z_send.at[k, step - 1],
                self.z_recv.at[k, step - 1],
                (lax.rem(self.z + step, self.depth), self.x, self.y, self.core),
            )
            for step in range(1, self.depth)
        ]

    def x_copy(self, k):
        full, lead, rows, cols = self.part(k)
        here = full.at[:, self.x, lead, rows, cols]
        return remote(here, here, self.x_send.at[k], self.x_recv.at[k], (self.z, 1 - self.x, self.y, self.core))

    def y_copy(self, k):
        full, lead, rows, cols = self.part(k)
        here = full.at[:, :, lead, rows, cols]
        return remote(here, here, self.y_send.at[k], self.y_recv.at[k], (self.z, self.x, 1 - self.y, self.core))

    def c_copy(self, k):
        full, lead, _, cols = self.part(k)
        here = full.at[:, :, lead, core_rows(full.shape[3], self.core), cols]
        return remote(here, here, self.c_send.at[k], self.c_recv.at[k], (self.z, self.x, self.y, 1 - self.core))

    def place_all(self):
        for k in range(self.count):
            self.place(k).start()

    def launch(self, k):
        if k < self.count:
            self.place(k).wait()
            for copy in self.z_copies(k):
                copy.start()

    def begin(self):
        for k in range(self.AHEAD):
            self.launch(k)

    def z_step(self):
        k, self.z_next = self.z_next, self.z_next + 1
        for copy in self.z_copies(k):
            copy.wait_recv()
        self.x_copy(k).start()
        self.launch(k + self.AHEAD)

    def x_step(self):
        k, self.x_next = self.x_next, self.x_next + 1
        self.x_copy(k).wait_recv()
        (self.c_copy if GATHER_CHUNKS[k][3] else self.y_copy)(k).start()

    def y_step(self):
        k, self.y_next = self.y_next, self.y_next + 1
        if not GATHER_CHUNKS[k][3]:
            self.y_copy(k).wait_recv()
            self.c_copy(k).start()

    def c_step(self):
        k, self.c_next = self.c_next, self.c_next + 1
        self.c_copy(k).wait_recv()

    def tick(self, upto=-1):
        count = self.count
        if self.z_next < count:
            self.z_step()
        for before, after, step, lag in (
            (self.z_next, self.x_next, self.x_step, 1),
            (self.x_next, self.y_next, self.y_step, 1),
            (self.y_next, self.c_next, self.c_step, 1),
        ):
            if after < before and (before - after > lag or before == count or after <= upto):
                step()

    def pump(self, ticks=1):
        for _ in range(ticks):
            if self.c_next < self.count:
                self.tick()

    def ready(self, tensor):
        last = max(k for k, chunk in enumerate(GATHER_CHUNKS) if chunk[0] == tensor)
        while self.c_next <= last:
            self.tick(last)

    def close(self):
        for k in range(self.count):
            for copy in self.z_copies(k):
                copy.wait_send()
            self.x_copy(k).wait_send()
            if not GATHER_CHUNKS[k][3]:
                self.y_copy(k).wait_send()
            self.c_copy(k).wait_send()


def taps(tensor):
    pieces = []
    for lead in (0, 3, 6):
        pieces += [(tensor, lead, 1, True, column, 256) for column in (0, 256)]
        pieces += [(tensor, lead + 1, 1, False, 0, 512), (tensor, lead + 2, 1, False, 0, 512)]
    return pieces


def blocks(tensor, leads, both):
    return [(tensor, lead, 1, lead in both, column, 128) for lead in leads for column in (0, 128)]


CHUNKS = (
    [(0, 0, 1, False, column, 512) for column in (0, 512)],
    taps(1),
    blocks(2, (0, 1), ()),
    blocks(3, (0, 1, 2, 3), (0,)),
    [
        (4, 0, 1, width == 256, column, width)
        for column, width in ((0, 256), (256, 256), (512, 512), (1024, 256), (1280, 256), (1536, 512))
    ],
    taps(5),
    blocks(6, (0, 1), ()),
)
GATHER_CHUNKS = [chunk for tensor in (0, 1, 3, 2, 4, 5, 6) for chunk in CHUNKS[tensor]]
REDUCE_CHUNKS = [chunk for tensor in (6, 5, 4, 2, 3, 1, 0) for chunk in CHUNKS[tensor]]


def add_blocks(extents, body):
    total = 1
    for extent in extents:
        total *= extent

    def step(flat, carry):
        index = []
        for extent in reversed(extents):
            index.append(lax.rem(flat, extent))
            flat = flat // extent
        body(*reversed(index))
        return carry

    lax.fori_loop(0, total, step, 0)


def add_to(target, source):
    target[...] = (target[...].astype(jnp.float32) + source[...].astype(jnp.float32)).astype(jnp.bfloat16)


class Reduce:
    def __init__(self, held, outs, c_hbm, y_hbm, refs, depth):
        self.held, self.outs, self.c_hbm, self.y_hbm, self.depth = held, outs, c_hbm, y_hbm, depth
        self.count = len(REDUCE_CHUNKS)
        refs = list(refs)

        def take(count):
            taken = refs[:count]
            del refs[:count]
            return taken

        self.from_x, self.from_z, self.swap = take(self.count), take(self.count), take(self.count)
        self.final = take(self.count)
        self.c_tall, self.c_wide, self.y_tall, self.y_wide, self.squares = take(5)
        self.c_sem, self.y_sem, self.x_sem, self.z_sem, self.s_sem, self.f_sem, self.q_sem, self.local_sem = take(8)
        self.z, self.x, self.y, self.core = position()
        self.enabled = 0
        self.next = [0] * len(self.LAGS)

    @staticmethod
    def sizes(shapes):
        for tensor, _, leads, both, _, columns in REDUCE_CHUNKS:
            rows = shapes[tensor][3]
            yield leads, rows, columns, rows // 2 if both else rows // 4, both

    @staticmethod
    def scratch(shapes, depth):
        dma, count = pltpu.SemaphoreType.DMA, len(REDUCE_CHUNKS)
        buffer = lambda *shape: pltpu.VMEM(shape, jnp.bfloat16)
        sizes = list(Reduce.sizes(shapes))
        return (
            [buffer(depth, leads, part, columns) for leads, _, columns, part, _ in sizes]
            + [buffer(depth - 1, leads, part, columns) for leads, _, columns, part, _ in sizes]
            + [buffer(leads, part, columns) if both else buffer(16, 128) for leads, _, columns, part, both in sizes]
            + [buffer(leads, rows, columns) for leads, rows, columns, _, _ in sizes]
            + [buffer(2, depth, 2, 1, shapes[2][3] // 2, 128), buffer(2, depth, 2, 1, shapes[0][3] // 2, 512)]
            + [buffer(2, depth, 2, 1, shapes[2][3] // 4, 128), buffer(2, depth, 2, 1, shapes[0][3] // 4, 512)]
            + [pltpu.VMEM((2 * depth + 3, 8, 128), jnp.float32)]
            + [dma((2, count))] * 3
            + [dma((2, count, depth - 1)), dma((2, count)), dma((2, count, 3)), dma((2, depth)), dma((3, count))]
        )

    def piece(self, k):
        tensor, lead, leads, both, column, columns = REDUCE_CHUNKS[k]
        held = self.held[tensor]
        rows = held.shape[3]
        return held, rows, pl.ds(lead, leads), pl.ds(column, columns), chunk_rows(rows, both, self.y, self.core)

    def extents(self, k):
        return REDUCE_CHUNKS[k][2], REDUCE_CHUNKS[k][1]

    def slot(self, k, tall, wide):
        tensor, columns = REDUCE_CHUNKS[k][0], REDUCE_CHUNKS[k][5]
        buffer = tall if tensor in (2, 3, 6) else wide
        return buffer.at[k % 2, :, :, :, :, pl.ds(0, columns)]

    def c_copy(self, k):
        held, rows, lead, cols, _ = self.piece(k)
        return remote(
            held.at[:, :, lead, core_rows(rows, 1 - self.core), cols],
            self.c_hbm[REDUCE_CHUNKS[k][0]].at[:, :, lead, :, cols],
            self.c_sem.at[0, k],
            self.c_sem.at[1, k],
            (self.z, self.x, self.y, 1 - self.core),
        )

    def c_load(self, k):
        _, _, lead, cols, _ = self.piece(k)
        return pltpu.make_async_copy(
            self.c_hbm[REDUCE_CHUNKS[k][0]].at[:, :, lead, :, cols],
            self.slot(k, self.c_tall, self.c_wide),
            self.local_sem.at[0, k],
        )

    def y_copy(self, k):
        held, rows, lead, cols, _ = self.piece(k)
        return remote(
            held.at[:, :, lead, chunk_rows(rows, False, 1 - self.y, self.core), cols],
            self.y_hbm[REDUCE_CHUNKS[k][0]].at[:, :, lead, :, cols],
            self.y_sem.at[0, k],
            self.y_sem.at[1, k],
            (self.z, self.x, 1 - self.y, self.core),
        )

    def y_load(self, k):
        _, _, lead, cols, _ = self.piece(k)
        return pltpu.make_async_copy(
            self.y_hbm[REDUCE_CHUNKS[k][0]].at[:, :, lead, :, cols],
            self.slot(k, self.y_tall, self.y_wide),
            self.local_sem.at[1, k],
        )

    def x_copy(self, k):
        held, _, lead, cols, rows = self.piece(k)
        return remote(
            held.at[:, 1 - self.x, lead, rows, cols],
            self.from_x[k],
            self.x_sem.at[0, k],
            self.x_sem.at[1, k],
            (self.z, 1 - self.x, self.y, self.core),
        )

    def z_copies(self, k):
        held, _, lead, cols, rows = self.piece(k)
        copies = []
        for step in range(1, self.depth):
            there = lax.rem(self.z + step, self.depth)
            copies.append(
                remote(
                    held.at[there, self.x, lead, rows, cols],
                    self.from_z[k].at[step - 1],
                    self.z_sem.at[0, k, step - 1],
                    self.z_sem.at[1, k, step - 1],
                    (there, self.x, self.y, self.core),
                )
            )
        return copies

    def s_copy(self, k):
        rows = self.piece(k)[4]
        return remote(
            self.final[k].at[:, rows],
            self.swap[k],
            self.s_sem.at[0, k],
            self.s_sem.at[1, k],
            (self.z, self.x, 1 - self.y, self.core),
        )

    def f_copies(self, k):
        here = self.final[k].at[:, self.piece(k)[4]]
        peers = [(self.z, self.x, self.y, 1 - self.core)]
        if not REDUCE_CHUNKS[k][3]:
            peers += [(self.z, self.x, 1 - self.y, self.core), (self.z, self.x, 1 - self.y, 1 - self.core)]
        return [
            remote(here, here, self.f_sem.at[0, k, i], self.f_sem.at[1, k, i], peer) for i, peer in enumerate(peers)
        ]

    def store(self, k):
        tensor = REDUCE_CHUNKS[k][0]
        _, _, lead, cols, _ = self.piece(k)
        return pltpu.make_async_copy(self.final[k], self.outs[tensor].at[lead, :, cols], self.local_sem.at[2, k])

    def add_c(self, k):
        held, rows, _, cols, _ = self.piece(k)
        leads, lead = self.extents(k)
        half, slot = core_rows(rows, self.core), self.slot(k, self.c_tall, self.c_wide)
        add_blocks(
            (self.depth, 2, leads), lambda z, x, i: add_to(held.at[z, x, lead + i, half, cols], slot.at[z, x, i])
        )

    def add_y(self, k):
        held, _, _, cols, rows = self.piece(k)
        leads, lead = self.extents(k)
        slot = self.slot(k, self.y_tall, self.y_wide)
        add_blocks(
            (self.depth, 2, leads), lambda z, x, i: add_to(held.at[z, x, lead + i, rows, cols], slot.at[z, x, i])
        )

    def add_x(self, k):
        held, _, _, cols, rows = self.piece(k)
        leads, lead = self.extents(k)
        add_blocks(
            (self.depth, leads), lambda z, i: add_to(held.at[z, self.x, lead + i, rows, cols], self.from_x[k].at[z, i])
        )

    def add_z(self, k):
        held, _, _, cols, rows = self.piece(k)
        leads, lead = self.extents(k)

        def body(i):
            total = held[self.z, self.x, lead + i, rows, cols].astype(jnp.float32)
            for step in range(1, self.depth):
                total = total + self.from_z[k][step - 1, i].astype(jnp.float32)
            self.final[k][i, rows] = total.astype(jnp.bfloat16)

        add_blocks((leads,), body)

    def add_s(self, k):
        rows = self.piece(k)[4]
        add_blocks((self.extents(k)[0],), lambda i: add_to(self.final[k].at[i, rows], self.swap[k].at[i]))

    def add_squares(self, k):
        leads = self.extents(k)[0]
        lanes = lax.broadcasted_iota(jnp.int32, (8, 128), 1)
        subs = lax.broadcasted_iota(jnp.int32, (8, 128), 0)
        where = (subs == 1) & (lanes == REDUCE_CHUNKS[k][0])

        def body(i):
            block = self.final[k][i].astype(jnp.float32)
            total = jnp.sum(jnp.sum(block * block, axis=0, keepdims=True), axis=1, keepdims=True)
            self.squares[2 * self.depth + 2] += jnp.where(where, total, 0.0)

        add_blocks((leads,), body)

    LAGS = (0, 1, 1, 1, 1, 1, 1, 1, 1)

    def stage(self, k, number):
        both = REDUCE_CHUNKS[k][3]
        if number == 0:
            self.c_copy(k).start()
        elif number == 1:
            self.c_copy(k).wait_recv()
            self.c_load(k).start()
        elif number == 2:
            self.c_load(k).wait()
            self.add_c(k)
            (self.x_copy if both else self.y_copy)(k).start()
        elif number == 3 and not both:
            self.y_copy(k).wait_recv()
            self.y_load(k).start()
        elif number == 4 and not both:
            self.y_load(k).wait()
            self.add_y(k)
            self.x_copy(k).start()
        elif number == 5:
            self.x_copy(k).wait_recv()
            self.add_x(k)
            for copy in self.z_copies(k):
                copy.start()
        elif number == 6:
            for copy in self.z_copies(k):
                copy.wait_recv()
            self.add_z(k)
            for copy in [self.s_copy(k)] if both else self.f_copies(k):
                copy.start()
        elif number == 7 and both:
            self.s_copy(k).wait_recv()
            self.s_copy(k).wait_send()
            self.add_s(k)
            for copy in self.f_copies(k):
                copy.start()
        elif number == 8:
            for copy in self.f_copies(k):
                copy.wait_recv()
            self.store(k).start()
            self.add_squares(k)

    def enable(self, tensor, leads_done=None):
        while self.enabled < self.count:
            chunk = REDUCE_CHUNKS[self.enabled]
            if chunk[0] != tensor or (leads_done is not None and chunk[1] + chunk[2] > leads_done):
                break
            self.enabled += 1

    def pump(self, ticks=1):
        for _ in range(ticks):
            for number in reversed(range(len(self.LAGS))):
                before = self.next[number - 1] if number else self.enabled
                behind = before - self.next[number]
                if behind > 0 and (behind > self.LAGS[number] or before == self.count):
                    self.stage(self.next[number], number)
                    self.next[number] += 1

    def finish(self, weight_squares, sums_out):
        while self.next[-1] < self.count:
            self.pump()
        squares, depth = self.squares, self.depth
        subs = lax.broadcasted_iota(jnp.int32, (8, 128), 0)
        mine = squares.at[self.z * 2 + self.x]
        mine[...] = squares[2 * depth + 2] + jnp.where(subs == 0, weight_squares[...], 0.0)
        copies = [
            remote(
                mine,
                mine,
                self.q_sem.at[0, step],
                self.q_sem.at[1, step],
                (lax.rem(self.z + step, depth), self.x, self.y, self.core),
            )
            for step in range(1, depth)
        ]
        for copy in copies:
            copy.start()
        for copy in copies:
            copy.wait_recv()
        own = squares[self.x]
        for deep in range(1, depth):
            own = own + squares[deep * 2 + self.x]
        column = squares.at[2 * depth + self.x]
        column[...] = own
        across = remote(
            column, column, self.q_sem.at[0, 0], self.q_sem.at[1, 0], (self.z, 1 - self.x, self.y, self.core)
        )
        across.start()
        across.wait_recv()
        sums_out[...] = squares[2 * depth] + squares[2 * depth + 1]
        across.wait_send()
        for copy in copies:
            copy.wait_send()
        for k in range(self.count):
            self.c_copy(k).wait_send()
            if not REDUCE_CHUNKS[k][3]:
                self.y_copy(k).wait_send()
            self.x_copy(k).wait_send()
            for copy in self.z_copies(k) + self.f_copies(k):
                copy.wait_send()
            self.store(k).wait()


class NearFar:
    def __init__(self, refs, depth):
        self.near, self.far, self.total, self.near_send, self.near_recv, self.far_send, self.far_recv = refs
        self.depth = depth
        self.z, self.x, self.y, self.core = position()
        self.mine = self.x * 4 + self.y * 2 + self.core
        self.pay = self.near.at[self.mine]
        self.sent = []

    @staticmethod
    def scratch(width, depth):
        dma = pltpu.SemaphoreType.DMA
        return [
            pltpu.VMEM((8, 8, width), jnp.float32),
            pltpu.VMEM((depth, 8, width), jnp.float32),
            pltpu.VMEM((8, width), jnp.float32),
            dma((7,)),
            dma((7,)),
            dma((depth - 1,)),
            dma((depth - 1,)),
        ]

    def near_copies(self):
        copies = []
        for offset in range(1, 8):
            x = 1 - self.x if offset & 4 else self.x
            y = 1 - self.y if offset & 2 else self.y
            core = 1 - self.core if offset & 1 else self.core
            here = self.near.at[self.mine]
            copies.append(
                remote(here, here, self.near_send.at[offset - 1], self.near_recv.at[offset - 1], (self.z, x, y, core))
            )
        return copies

    def far_copies(self):
        here = self.far.at[self.z]
        return [
            remote(
                here,
                here,
                self.far_send.at[step - 1],
                self.far_recv.at[step - 1],
                (lax.rem(self.z + step, self.depth), self.x, self.y, self.core),
            )
            for step in range(1, self.depth)
        ]

    def begin(self):
        for copy in self.near_copies():
            copy.start()

    def stages(self):
        def middle():
            for copy in self.near_copies():
                copy.wait_recv()
            total = self.near[0]
            for slot in range(1, 8):
                total = total + self.near[slot]
            self.far[self.z] = total
            for copy in self.far_copies():
                copy.start()

        def last():
            for copy in self.far_copies():
                copy.wait_recv()
            total = self.far[0]
            for slot in range(1, self.depth):
                total = total + self.far[slot]
            self.total[...] = total

        return [middle, last]

    def close(self):
        for copy in self.near_copies() + self.far_copies():
            copy.wait_send()


class Split:
    def __init__(self, refs, depth):
        (self.pay, self.half, self.quad, self.deep, self.total, self.c_send, self.c_recv) = refs[:7]
        (self.q_send, self.q_recv, self.z_send, self.z_recv, self.g_send, self.g_recv) = refs[7:]
        self.depth = depth
        self.z, self.x, self.y, self.core = position()
        self.width = self.pay.shape[1]
        self.mine = self.x * 2 + self.y

    @staticmethod
    def scratch(width, depth):
        dma = pltpu.SemaphoreType.DMA
        return [
            pltpu.VMEM((8, width), jnp.float32),
            pltpu.VMEM((8, width // 2), jnp.float32),
            pltpu.VMEM((4, 8, width // 8), jnp.float32),
            pltpu.VMEM((depth, 8, width // 8), jnp.float32),
            pltpu.VMEM((8, width), jnp.float32),
            dma((2,)),
            dma((2,)),
            dma((3,)),
            dma((3,)),
            dma((depth - 1,)),
            dma((depth - 1,)),
            dma((3,)),
            dma((3,)),
        ]

    def half_of(self, core):
        return pl.ds(pl.multiple_of(core * (self.width // 2), 128), self.width // 2)

    def eighth_of(self, slot):
        start = self.core * (self.width // 2) + slot * (self.width // 8)
        return pl.ds(pl.multiple_of(start, 128), self.width // 8)

    def core_copy(self):
        return remote(
            self.pay.at[:, self.half_of(1 - self.core)],
            self.half,
            self.c_send.at[0],
            self.c_recv.at[0],
            (self.z, self.x, self.y, 1 - self.core),
        )

    def around(self):
        for offset in range(1, 4):
            x = 1 - self.x if offset & 2 else self.x
            y = 1 - self.y if offset & 1 else self.y
            yield offset - 1, x, y

    def quad_copies(self):
        return [
            remote(
                self.pay.at[:, self.eighth_of(x * 2 + y)],
                self.quad.at[self.mine],
                self.q_send.at[i],
                self.q_recv.at[i],
                (self.z, x, y, self.core),
            )
            for i, x, y in self.around()
        ]

    def deep_copies(self):
        here = self.deep.at[self.z]
        return [
            remote(
                here,
                here,
                self.z_send.at[step - 1],
                self.z_recv.at[step - 1],
                (lax.rem(self.z + step, self.depth), self.x, self.y, self.core),
            )
            for step in range(1, self.depth)
        ]

    def gather_copies(self):
        here = self.total.at[:, self.eighth_of(self.mine)]
        return [
            remote(here, here, self.g_send.at[i], self.g_recv.at[i], (self.z, x, y, self.core))
            for i, x, y in self.around()
        ]

    def last_copy(self):
        here = self.total.at[:, self.half_of(self.core)]
        return remote(here, here, self.c_send.at[1], self.c_recv.at[1], (self.z, self.x, self.y, 1 - self.core))

    def begin(self):
        self.core_copy().start()

    def stages(self):
        def first():
            self.core_copy().wait_recv()
            half = self.half_of(self.core)
            self.pay[:, half] = self.pay[:, half] + self.half[...]
            for copy in self.quad_copies():
                copy.start()
            self.quad[self.mine] = self.pay[:, self.eighth_of(self.mine)]

        def second():
            for copy in self.quad_copies():
                copy.wait_recv()
            self.deep[self.z] = (self.quad[0] + self.quad[1]) + (self.quad[2] + self.quad[3])
            for copy in self.deep_copies():
                copy.start()

        def third():
            for copy in self.deep_copies():
                copy.wait_recv()
            total = self.deep[0]
            for slot in range(1, self.depth):
                total = total + self.deep[slot]
            self.total[:, self.eighth_of(self.mine)] = total
            for copy in self.gather_copies():
                copy.start()

        def fourth():
            for copy in self.gather_copies():
                copy.wait_recv()
            self.last_copy().start()

        def fifth():
            self.last_copy().wait_recv()
            for copy in self.gather_copies() + [self.last_copy()]:
                copy.wait_send()

        return [first, second, third, fourth, fifth]

    def close(self):
        self.core_copy().wait_send()
        for copy in self.quad_copies() + self.deep_copies():
            copy.wait_send()


def interleave(stages, works):
    done = 0
    for i, stage in enumerate(stages):
        upto = (len(works) * (i + 1)) // len(stages)
        for work in works[done:upto]:
            work()
        done = upto
        stage()


HAT_A1, HAT_A2, HAT_A3, HAT_AS, HAT_B1, HAT_B2, HAT_B3, PATCH_A, PATCH_B, ACT_A2, ACT_B2, OUT_A = SAVED = range(12)
SUM_A1, SUM_A2, SUM_A3, SUM_AS, SUM_B1, SUM_B2, SUM_B3, SUM_J = range(8)


def paced(first, last, body, parts, pump):
    for part in range(parts):
        span = last - first
        lax.fori_loop(first + span * part // parts, first + span * (part + 1) // parts, body, 0)
        pump()


def columns(j):
    return pl.ds(pl.multiple_of(j * 128, 128), 128)


def dot(a, b):
    return lax.dot_general(a, b, (((1,), (0,)), ((), ())), preferred_element_type=jnp.float32)


def dot_nt(a, b):
    return lax.dot_general(a, b, (((1,), (1,)), ((), ())), preferred_element_type=jnp.float32)


def sigmoid(v):
    return 0.5 * jnp.tanh(0.5 * v) + 0.5


def slope(v):
    s = sigmoid(v)
    return s * (1.0 + v * (1.0 - s))


class Plan:
    def __init__(self, shapes):
        self.sides = [shape[1] // 2 for shape in shapes]
        self.slots = [shape[0] for shape in shapes]
        self.valid = [side * side * slots for side, slots in zip(self.sides, self.slots)]
        sizes = [-(-valid // 8) * 8 for valid in self.valid]
        sizes[2] += -sum(sizes) % 128
        self.starts = [0, sizes[0], sizes[0] + sizes[1]]
        self.sizes = sizes
        self.rows = sum(sizes)

    def spans(self):
        return [slice(start, start + size) for start, size in zip(self.starts, self.sizes)]

    def shifts(self):
        out = np.zeros((9, self.rows, self.rows), np.float32)
        for side, slots, start in zip(self.sides, self.slots, self.starts):
            at = lambda i, j, n: start + (i * side + j) * slots + n
            for di in (-1, 0, 1):
                for dj in (-1, 0, 1):
                    for i in range(max(0, -di), min(side, side - di)):
                        for j in range(max(0, -dj), min(side, side - dj)):
                            for n in range(slots):
                                out[(di + 1) * 3 + dj + 1, at(i, j, n), at(i + di, j + dj, n)] = 1.0
        return out.astype(jnp.bfloat16)


def put_sums(plan, pairs, mask, pay, base, width, pump=None):
    def body(j, carry):
        firsts, seconds = [0.0] * 3, [0.0] * 3
        for first, second in pairs(j):
            for g, span in enumerate(plan.spans()):
                live = first[span] * mask[span, :]
                firsts[g] = firsts[g] + jnp.sum(live, axis=0, keepdims=True)
                seconds[g] = seconds[g] + jnp.sum(live * second[span], axis=0, keepdims=True)
        zero = jnp.zeros((1, 128), jnp.float32)
        pay[:, columns(base + j)] = jnp.concatenate(firsts + seconds + [zero, zero], axis=0)
        return carry

    if pump is None:
        lax.fori_loop(0, width // 128, body, 0)
    else:
        paced(0, width // 128, body, 2, pump)


def put_scales(total, inverse, over, width, factor=1.0):
    def body(j, carry):
        at = columns(j)
        per = over[0:3, :] * factor
        means = total[0:3, at] * per
        variance = total[3:6, at] * per - means * means
        scales = lax.rsqrt(variance + EPSILON)
        zero = jnp.zeros((5, 128), jnp.float32)
        total[:, at] = jnp.concatenate([means, zero], axis=0)
        inverse[:, at] = jnp.concatenate([scales, zero], axis=0)
        return carry

    lax.fori_loop(0, width // 128, body, 0)


def by_group(plan, of):
    return jnp.concatenate([of(g, span) for g, span in enumerate(plan.spans())], axis=0)


def forward_names(depth):
    return (
        (SUM_A1, NearFar.scratch(512, depth)),
        (SUM_A2, NearFar.scratch(512, depth)),
        (SUM_AS, Split.scratch(2048, depth)),
        (SUM_A3, Split.scratch(2048, depth)),
        (SUM_B1, NearFar.scratch(512, depth)),
        (SUM_B2, NearFar.scratch(512, depth)),
        (SUM_B3, Split.scratch(2048, depth)),
    )


def forward_kernel(plan, depth, *refs):
    refs = list(refs)

    def take(count):
        taken = refs[:count]
        del refs[:count]
        return taken

    x_hbm, shift_hbm, mask, counts, norm_mid, norm_out = take(6)
    shards = take(7)
    out, inv_mid, inv_out, par_mid, par_out, over, weight_squares = take(7)
    weights_hbm = take(7)
    saved_hbm = dict(zip(SAVED, take(len(SAVED))))
    sums = {}
    for name, scratch in forward_names(depth):
        sums[name] = (NearFar if len(scratch) == 7 else Split)(take(len(scratch)), depth)
    x, shift = take(2)
    w_a1, w_a2, w_a3, w_as, w_b1, w_b2, w_b3 = weights = take(7)
    saved = dict(zip(SAVED, take(len(SAVED))))
    hid_a1, hid_mid, hid_out, hid_as, act = take(5)
    load_sem, save_sem, full_sem, norms_mid, norms_out, norm_send, norm_recv = take(7)
    gather = Gather(shards, weights, take(9), depth)

    loads = [
        pltpu.make_async_copy(src, dst, load_sem.at[i])
        for i, (src, dst) in enumerate(zip([x_hbm, shift_hbm], [x, shift]))
    ]
    gather.place_all()
    for copy in loads:
        copy.start()

    def keep(i):
        return pltpu.make_async_copy(weights[i], weights_hbm[i], full_sem.at[i])

    weight_squares[...] = jnp.zeros((8, 128), jnp.float32)

    def ready(i):
        gather.ready(i)
        keep(i).start()

    def add_square(i):
        at_row = lax.broadcasted_iota(jnp.int32, (8, 128), 0) == 0
        where = at_row & (lax.broadcasted_iota(jnp.int32, (8, 128), 1) == i)

        def body(lead, carry):
            block = weights[i][gather.z, gather.x, lead].astype(jnp.float32)
            total = jnp.sum(jnp.sum(block * block, axis=0, keepdims=True), axis=1, keepdims=True)
            weight_squares[...] += jnp.where(where, total, 0.0)
            return carry

        lax.fori_loop(0, weights[i].shape[2], body, 0)

    def pump():
        gather.pump()

    def save(name):
        pltpu.make_async_copy(saved[name], saved_hbm[name], save_sem.at[SAVED.index(name)]).start()

    greet(depth, crosswise=True)
    place = gather.z * 2 + gather.x
    norms_mid[place] = norm_mid[...]
    own_lanes = pl.ds(pl.multiple_of(place * norm_out.shape[1], 128), norm_out.shape[1])
    norms_out[:, own_lanes] = norm_out[...]

    def norm_copies(kind):
        here = norms_out.at[:, own_lanes] if kind else norms_mid.at[place]
        copies = []
        for i in range(1, 2 * depth):
            peer = (lax.rem(gather.z + i // 2, depth), 1 - gather.x if i % 2 else gather.x, gather.y, gather.core)
            copies.append(remote(here, here, norm_send.at[kind, i], norm_recv.at[kind, i], peer))
        return copies

    for copy in norm_copies(0) + norm_copies(1):
        copy.start()
    gather.begin()
    rows = plan.rows

    loads[0].wait()
    ready(0)

    def conv_a1(p, carry):
        hid_a1[p] = dot_nt(x[p], w_a1[...].reshape(512, -1))
        return carry

    paced(0, 2, conv_a1, 2, pump)
    paced(2, 4, conv_a1, 2, pump)

    total = sums[SUM_A1]
    put_sums(
        plan, lambda j: [(hid_a1[p, :, columns(j)],) * 2 for p in range(4)], mask, total.pay, 0, 512, pump
    )
    total.pay[6:7, 0:128] = counts[...]
    total.begin()
    add_square(0)
    pump()
    total.stages()[0]()
    pump()
    total.stages()[1]()
    for copy in norm_copies(0):
        copy.wait_recv()
    own_norms = norms_mid[0]
    for slot in range(1, 2 * depth):
        own_norms = own_norms + norms_mid[slot]
    par_mid[...] = own_norms

    pixels = total.total[6:7, 0:128]
    lanes = lax.broadcasted_iota(jnp.int32, (1, 128), 1)
    inverse_counts = [
        jnp.broadcast_to(1.0 / jnp.sum(jnp.where(lanes == g, pixels, 0.0), axis=1, keepdims=True), (1, 128))
        for g in range(3)
    ]
    over[...] = jnp.concatenate(inverse_counts + [jnp.zeros((5, 128), jnp.float32)], axis=0)
    put_scales(total.total, inv_mid.at[0], over, 512, 0.25)

    def normalized(hidden, total, inverse, hat, params, row, j):
        at = columns(j)
        xhat = by_group(plan, lambda g, span: (hidden[span] - total[g : g + 1, at]) * inverse[g : g + 1, at])
        hat[:, at] = xhat.astype(jnp.bfloat16)
        return xhat * params[row : row + 1, at] + params[row + 1 : row + 2, at]

    def activate(hidden_of, total, inverse, hat, params, row, target):
        def body(j, carry):
            v = normalized(hidden_of(j), total, inverse, hat, params, row, j)
            target[:, columns(j)] = (v * sigmoid(v)).astype(jnp.bfloat16)
            return carry

        lax.fori_loop(0, 4, body, 0)

    def activate_a1(p, carry):
        activate(
            lambda j: hid_a1[p, :, columns(j)],
            total.total,
            inv_mid.at[0],
            saved[HAT_A1].at[p],
            par_mid,
            0,
            act.at[p],
        )
        return carry

    paced(0, 4, activate_a1, 4, pump)
    save(HAT_A1)

    loads[1].wait()
    patch = saved[PATCH_A]
    for tap in range(9):
        a, b = tap // 3, tap % 3
        plane = (0 if a == 1 else 2) + (0 if b == 1 else 1)
        matrix = (0 if a == 0 else 1) * 3 + (0 if b == 0 else 1)
        if matrix == 4:
            patch[tap] = act[plane]
        else:
            patch[tap] = dot(shift[matrix], act[plane]).astype(jnp.bfloat16)
        if tap in (2, 5):
            pump()
    save(PATCH_A)
    ready(1)

    def spatial(patch, weight):
        hid_mid[...] = dot_nt(patch[0], weight[:, :, 0].reshape(512, 512))

        def body(tap, carry):
            hid_mid[...] += dot_nt(patch[tap], weight[:, :, tap].reshape(512, 512))
            return carry

        paced(1, 9, body, 3, pump)

    spatial(patch, w_a2)

    def conv_as(d, carry):
        at = pl.ds(pl.multiple_of(d * 256, 256), 256)
        hid_as[:, at] = dot(x[0], w_as[d // 2, lax.rem(d, 2)].reshape(1024, 256))
        return carry

    def shortcut():
        ready(3)
        paced(0, 8, conv_as, 2, pump)
        put_sums(plan, lambda j: [(hid_as[:, columns(j)],) * 2], mask, sums[SUM_AS].pay, 0, 2048, pump)
        sums[SUM_AS].begin()

    as_stages = sums[SUM_AS].stages()

    def mid_sums(total, name_index, works):
        put_sums(plan, lambda j: [(hid_mid[:, columns(j)],) * 2], mask, total.pay, 0, 512)
        total.begin()
        interleave(total.stages(), works)
        put_scales(total.total, inv_mid.at[name_index], over, 512)

    mid_sums(sums[SUM_A2], 1, [pump, lambda: add_square(1), pump])
    activate(
        lambda j: hid_mid[:, columns(j)], sums[SUM_A2].total, inv_mid.at[1], saved[HAT_A2], par_mid, 2, saved[ACT_A2]
    )
    save(HAT_A2)
    save(ACT_A2)

    def expand(act_ref, weight):
        def body(d, carry):
            at = pl.ds(pl.multiple_of(d * 256, 256), 256)
            hid_out[:, at] = dot(act_ref[...], weight[d // 2, lax.rem(d, 2)].reshape(512, 256))
            return carry

        paced(0, 8, body, 2, pump)

    def out_sums(total, name_index, works):
        put_sums(plan, lambda j: [(hid_out[:, columns(j)],) * 2], mask, total.pay, 0, 2048, pump)
        total.begin()
        interleave(total.stages(), works)
        put_scales(total.total, inv_out.at[name_index], over, 2048)

    shortcut()
    as_stages[0]()
    ready(2)
    as_stages[1]()
    expand(saved[ACT_A2], w_a3)
    as_stages[2]()
    out_sums(sums[SUM_A3], 0, [as_stages[3], pump, as_stages[4], pump, lambda: add_square(2), lambda: add_square(3), pump])
    put_scales(sums[SUM_AS].total, inv_out.at[1], over, 2048)

    for copy in norm_copies(1):
        copy.wait_recv()
    par_out[...] = norms_out[...]

    def join(j, carry):
        at = columns(j)
        v = normalized(hid_out[:, at], sums[SUM_A3].total, inv_out.at[0], saved[HAT_A3], par_out, 0, j)
        v = v + normalized(hid_as[:, at], sums[SUM_AS].total, inv_out.at[1], saved[HAT_AS], par_out, 2, j)
        saved[OUT_A][:, at] = (v * sigmoid(v) * mask[...]).astype(jnp.bfloat16)
        return carry

    paced(0, 16, join, 4, pump)
    for name in (HAT_A3, HAT_AS, OUT_A):
        save(name)

    ready(4)
    hid_mid[...] = dot_nt(saved[OUT_A][...], w_b1[...].reshape(512, -1))
    mid_sums(sums[SUM_B1], 2, [pump, lambda: add_square(4), pump])
    activate(
        lambda j: hid_mid[:, columns(j)], sums[SUM_B1].total, inv_mid.at[2], saved[HAT_B1], par_mid, 4, act.at[0]
    )
    save(HAT_B1)

    def patches(tap, carry):
        saved[PATCH_B][tap] = dot(shift[tap], act[0]).astype(jnp.bfloat16)
        return carry

    paced(0, 9, patches, 3, pump)
    save(PATCH_B)
    ready(5)
    spatial(saved[PATCH_B], w_b2)
    mid_sums(sums[SUM_B2], 3, [pump, lambda: add_square(5), pump])
    activate(
        lambda j: hid_mid[:, columns(j)], sums[SUM_B2].total, inv_mid.at[3], saved[HAT_B2], par_mid, 6, saved[ACT_B2]
    )
    save(HAT_B2)
    save(ACT_B2)
    ready(6)
    expand(saved[ACT_B2], w_b3)
    out_sums(sums[SUM_B3], 2, [lambda: add_square(6)])

    def finish(j, carry):
        at = columns(j)
        v = normalized(hid_out[:, at], sums[SUM_B3].total, inv_out.at[2], saved[HAT_B3], par_out, 4, j)
        v = v + saved[OUT_A][:, at].astype(jnp.float32)
        out[:, at] = (v * sigmoid(v) * mask[...]).astype(jnp.bfloat16)
        return carry

    lax.fori_loop(0, 16, finish, 0)
    save(HAT_B3)
    for total in sums.values():
        total.close()
    for i, name in enumerate(SAVED):
        pltpu.make_async_copy(saved[name], saved_hbm[name], save_sem.at[i]).wait()
    gather.close()
    for copy in norm_copies(0) + norm_copies(1):
        copy.wait_send()
    for i in range(7):
        keep(i).wait()


def saved_shapes(rows):
    bf16 = jnp.bfloat16
    return (
        ((4, rows, 512), bf16),
        ((rows, 512), bf16),
        ((rows, 2048), bf16),
        ((rows, 2048), bf16),
        ((rows, 512), bf16),
        ((rows, 512), bf16),
        ((rows, 2048), bf16),
        ((9, rows, 512), bf16),
        ((9, rows, 512), bf16),
        ((rows, 512), bf16),
        ((rows, 512), bf16),
        ((rows, 2048), bf16),
    )


WHOLE = pl.BlockSpec(memory_space=pltpu.VMEM)
VMEM_LIMIT = 62 * 1024 * 1024


def run_forward(plan, depth, x, shifts, mask, counts, norm_mid, norm_out, shards):
    rows, f32, bf16 = plan.rows, jnp.float32, jnp.bfloat16
    dma = pltpu.SemaphoreType.DMA
    scratch = []
    for _, pieces in forward_names(depth):
        scratch += pieces
    scratch += [pltpu.VMEM(x.shape, bf16), pltpu.VMEM(shifts.shape, bf16)]
    fulls = [jax.ShapeDtypeStruct((depth, 2, *shard.shape), bf16) for shard in shards]
    scratch += [pltpu.VMEM(full.shape, bf16) for full in fulls]
    scratch += [pltpu.VMEM(shape, kind) for shape, kind in saved_shapes(rows)]
    scratch += [
        pltpu.VMEM((4, rows, 512), f32),
        pltpu.VMEM((rows, 512), f32),
        pltpu.VMEM((rows, 2048), f32),
        pltpu.VMEM((rows, 2048), f32),
        pltpu.VMEM((4, rows, 512), bf16),
        dma((2,)),
        dma((len(SAVED),)),
        dma((7,)),
        pltpu.VMEM((2 * depth, 8, 512), f32),
        pltpu.VMEM((8, 2048), f32),
        dma((2, 2 * depth)),
        dma((2, 2 * depth)),
    ]
    scratch += Gather.scratch(depth)
    small = [
        jax.ShapeDtypeStruct((rows, 2048), bf16),
        jax.ShapeDtypeStruct((4, 8, 512), f32),
        jax.ShapeDtypeStruct((3, 8, 2048), f32),
        jax.ShapeDtypeStruct((8, 512), f32),
        jax.ShapeDtypeStruct((8, 2048), f32),
        jax.ShapeDtypeStruct((8, 128), f32),
        jax.ShapeDtypeStruct((8, 128), f32),
    ]
    return pl.pallas_call(
        functools.partial(forward_kernel, plan, depth),
        out_shape=small + fulls + [jax.ShapeDtypeStruct(shape, kind) for shape, kind in saved_shapes(rows)],
        in_specs=[ANY, ANY] + [WHOLE] * 4 + [ANY] * 7,
        out_specs=[WHOLE] * 7 + [ANY] * 7 + [ANY] * len(SAVED),
        scratch_shapes=scratch,
        compiler_params=pltpu.CompilerParams(collective_id=0, has_side_effects=True, vmem_limit_bytes=VMEM_LIMIT),
    )(x, shifts, mask, counts, norm_mid, norm_out, *shards)


def backward_names(depth):
    return (
        (SUM_B3, Split.scratch(2048, depth)),
        (SUM_B2, NearFar.scratch(512, depth)),
        (SUM_B1, NearFar.scratch(512, depth)),
        (SUM_J, Split.scratch(4096, depth)),
        (SUM_A2, NearFar.scratch(512, depth)),
        (SUM_A1, NearFar.scratch(512, depth)),
    )


def backward_kernel(plan, depth, *refs):
    refs = list(refs)

    def take(count):
        taken = refs[:count]
        del refs[:count]
        return taken

    x_hbm, shift_hbm, cot_hbm, mask, weight_squares, inv_mid, inv_out, par_mid, par_out, over = take(10)
    saved_hbm = dict(zip(SAVED, take(len(SAVED))))
    weights_hbm = take(7)
    dx_hbm, pgrad_mid, pgrad_b3, pgrad_j, squares_out = take(5)
    gradients_hbm, c_hbm, y_hbm = take(7), take(7), take(7)
    sums = {}
    for name, scratch in backward_names(depth):
        sums[name] = (NearFar if len(scratch) == 7 else Split)(take(len(scratch)), depth)
    x, shift, cot = take(3)
    w_a1, w_a2, w_a3, w_as, w_b1, w_b2, w_b3 = weights = take(7)
    kept = [name for name in SAVED if name != PATCH_B]
    saved = dict(zip(kept, take(len(kept))))
    saved[PATCH_B] = saved[PATCH_A]
    dz, dact, dh_mid, flip = take(4)
    load_sem, saved_sem, dx_sem = take(3)
    dh_a, dh_b = cot, saved[HAT_B3]
    planes = [saved[HAT_AS].at[:, pl.ds(plane * 512, 512)] for plane in range(4)]
    reduce = Reduce(weights, gradients_hbm, c_hbm, y_hbm, refs, depth)
    reduce.squares[2 * depth + 2] = jnp.zeros((8, 128), jnp.float32)

    def pump():
        reduce.pump()

    def loading(name):
        return pltpu.make_async_copy(saved_hbm[name], saved[name], saved_sem.at[SAVED.index(name)])

    loads = [
        pltpu.make_async_copy(src, dst, load_sem.at[i])
        for i, (src, dst) in enumerate(zip([x_hbm, shift_hbm, cot_hbm, *weights_hbm], [x, shift, cot, *weights]))
    ]
    first = (HAT_B3, OUT_A)
    for name in first:
        loading(name).start()
    loads[2].start()
    order = (HAT_B2, ACT_B2, HAT_B1, PATCH_B, HAT_A3, HAT_AS, HAT_A2, ACT_A2, HAT_A1)
    loads[9].start()
    for name in order[:4]:
        loading(name).start()
    for i in (1, 8, 7):
        loads[i].start()
    for name in order[4:]:
        loading(name).start()
    for i in (5, 6, 4, 0, 3):
        loads[i].start()

    greet(depth)

    def quarter(d):
        return pl.ds(pl.multiple_of(d * 256, 256), 256)

    def affine(hat, params, row, at):
        return hat[:, at].astype(jnp.float32) * params[row : row + 1, at] + params[row + 1 : row + 2, at]

    def norm_back(dz_of, hat, total, base, inverse, params, row, target, blocks):
        def body(j, carry):
            at = columns(j)
            sums_at = columns(base + j)
            gain = params[row : row + 1, at]
            value, xhat = dz_of(j), hat[:, at].astype(jnp.float32)

            def of(g, span):
                first = total[g : g + 1, sums_at] * over_of(g)
                second = total[3 + g : 4 + g, sums_at] * over_of(g)
                return (gain * inverse[g : g + 1, at]) * (value[span] - first - xhat[span] * second)

            target[:, at] = (by_group(plan, of) * mask[...]).astype(jnp.bfloat16)
            return carry

        paced(0, blocks, body, 1 if blocks == 4 else 2, pump)

    scale = [1.0]

    def over_of(g):
        return over[g : g + 1, :] * scale[0]

    for name in first:
        loading(name).wait()
    loads[2].wait()

    def out_pairs(j):
        at = columns(j)
        v = affine(saved[HAT_B3], par_out, 4, at) + saved[OUT_A][:, at].astype(jnp.float32)
        value = cot[:, at].astype(jnp.float32) * mask[...] * slope(v)
        dz[:, at] = value
        return [(value, saved[HAT_B3][:, at].astype(jnp.float32))]

    total = sums[SUM_B3]
    put_sums(plan, out_pairs, mask, total.pay, 0, 2048)
    total.begin()
    for i in (9, 1, 8, 7):
        loads[i].wait()
    for name in order[:4]:
        loading(name).wait()
    flip[0:512] = saved[ACT_B2][...].T
    interleave(total.stages(), [])
    pgrad_b3[...] = total.total[...]
    norm_back(lambda j: dz[:, columns(j)], saved[HAT_B3], total.total, 0, inv_out.at[2], par_out, 4, dh_a, 16)

    def contract(dh, weight):
        dact[...] = dot_nt(dh[:, 0:256], weight[0, 0].reshape(512, 256))

        def body(d, carry):
            dact[...] += dot_nt(dh[:, quarter(d)], weight[d // 2, lax.rem(d, 2)].reshape(512, 256))
            return carry

        paced(1, 8, body, 2, pump)

    def expand_term(lhs, dh, weight, first_slot, last_slot):
        def body(d, carry):
            shape = weight.shape[2:]
            weight[d // 2, lax.rem(d, 2)] = dot(lhs, dh[:, quarter(d)]).astype(jnp.bfloat16).reshape(shape)
            return carry

        lax.fori_loop(first_slot, last_slot, body, 0)

    def mid_pairs(hat, row):
        def pairs(j):
            at = columns(j)
            value = dact[:, at] * slope(affine(saved[hat], par_mid, row, at))
            dact[:, at] = value
            return [(value, saved[hat][:, at].astype(jnp.float32))]

        return pairs

    def mid_norm(name, hat, index, row, works):
        total = sums[name]
        put_sums(plan, mid_pairs(hat, row), mask, total.pay, 0, 512, pump)
        total.begin()
        interleave(total.stages(), works)
        pgrad_mid[index] = total.total[...]
        norm_back(lambda j: dact[:, columns(j)], saved[hat], total.total, 0, inv_mid.at[index], par_mid, row, dh_mid, 4)

    contract(dh_a, w_b3)

    def third_term(part):
        def work():
            expand_term(flip[0:512, :], dh_a, w_b3, 4 * part, 4 * part + 4)
            if part:
                reduce.enable(6)
                pump()

        return work

    mid_norm(SUM_B2, HAT_B2, 3, 6, [third_term(0), third_term(1)])

    def spread(tap, carry):
        part = dot(
            dot(shift[8 - tap], dh_mid[...]).astype(jnp.bfloat16), w_b2[:, :, tap].reshape(512, 512)
        )
        dact[...] = part + jnp.where(tap == 0, 0.0, dact[...])
        return carry

    paced(0, 9, spread, 5, pump)
    flip[0:512] = dh_mid[...].T

    def spatial_term(weight, patch, first_tap, last_tap, tensor):
        def work():
            def body(tap, carry):
                weight[:, :, tap] = dot(flip[0:512, :], patch[tap]).astype(jnp.bfloat16).reshape(depth, 2, 64, 512)
                return carry

            lax.fori_loop(first_tap, last_tap, body, 0)
            reduce.enable(tensor, last_tap)
            pump()

        return work

    mid_norm(
        SUM_B1,
        HAT_B1,
        2,
        4,
        [spatial_term(w_b2, saved[PATCH_B], 0, 3, 5), spatial_term(w_b2, saved[PATCH_B], 3, 6, 5)],
    )
    spatial_term(w_b2, saved[PATCH_B], 6, 9, 5)()
    loading(PATCH_A).start()

    def residual(d, carry):
        at = quarter(d)
        dz[:, at] = dz[:, at] + dot(dh_mid[...], w_b1[:, :, 0, :, at].reshape(512, 256))
        return carry

    paced(0, 8, residual, 2, pump)
    for name in order[4:]:
        loading(name).wait()

    def join_pairs(j):
        at = columns(j)
        v = affine(saved[HAT_A3], par_out, 0, at) + affine(saved[HAT_AS], par_out, 2, at)
        value = dz[:, at] * mask[...] * slope(v)
        dz[:, at] = value
        return [(value, saved[HAT_A3][:, at].astype(jnp.float32))]

    total = sums[SUM_J]
    put_sums(plan, join_pairs, mask, total.pay, 0, 2048, pump)
    put_sums(
        plan, lambda j: [(dz[:, columns(j)], saved[HAT_AS][:, columns(j)].astype(jnp.float32))], mask, total.pay, 16, 2048, pump
    )
    total.begin()
    flip[0:512] = dh_mid[...].T

    def first_term(part):
        def work():
            def body(d, carry):
                at = quarter(d)
                value = dot(flip[0:512, :], saved[OUT_A][:, at]).astype(jnp.bfloat16)
                w_b1[:, :, 0, :, at] = value.reshape(depth, 2, 64, 256)
                return carry

            lax.fori_loop(2 * part, 2 * part + 2, body, 0)
            if part == 3:
                reduce.enable(4)
            pump()

        return work

    interleave(total.stages(), [first_term(part) for part in range(4)])
    pgrad_j[...] = total.total[...]
    norm_back(lambda j: dz[:, columns(j)], saved[HAT_A3], total.total, 0, inv_out.at[0], par_out, 0, dh_a, 16)
    pump()
    norm_back(lambda j: dz[:, columns(j)], saved[HAT_AS], total.total, 16, inv_out.at[1], par_out, 2, dh_b, 16)
    for i in (5, 6, 4, 0, 3):
        loads[i].wait()

    pump()
    contract(dh_a, w_a3)
    pump()
    flip[0:512] = saved[ACT_A2][...].T

    def third_term_a():
        expand_term(flip[0:512, :], dh_a, w_a3, 0, 4)
        pump()
        expand_term(flip[0:512, :], dh_a, w_a3, 4, 8)
        reduce.enable(2)
        pump()

    def shortcut():
        even = dz.at[:, 0:1024]
        even[...] = dot_nt(dh_b[:, 0:256], w_as[0, 0].reshape(1024, 256))

        def body(d, carry):
            even[...] += dot_nt(dh_b[:, quarter(d)], w_as[d // 2, lax.rem(d, 2)].reshape(1024, 256))
            return carry

        paced(1, 8, body, 3, pump)

        def keep(j, carry):
            value = even[:, columns(j)]
            high = value.astype(jnp.bfloat16)
            saved[OUT_A][:, columns(j)] = high
            saved[OUT_A][:, columns(8 + j)] = (value - high.astype(jnp.float32)).astype(jnp.bfloat16)
            return carry

        lax.fori_loop(0, 8, keep, 0)

    mid_norm(SUM_A2, HAT_A2, 1, 2, [third_term_a, shortcut])

    loading(PATCH_A).wait()
    flip[...] = x[0].T
    for part in range(4):
        expand_term(flip[...], dh_b, w_as, 2 * part, 2 * part + 2)
        pump()
    reduce.enable(3)
    for plane in range(4):
        at = slice(plane * 512, plane * 512 + 512)
        begun = False
        for tap in range(9):
            a, b = tap // 3, tap % 3
            if plane != (0 if a == 1 else 2) + (0 if b == 1 else 1):
                continue
            matrix = (2 if a == 0 else 1) * 3 + (2 if b == 0 else 1)
            moved = dh_mid[...] if matrix == 4 else dot(shift[matrix], dh_mid[...]).astype(jnp.bfloat16)
            part = dot(moved, w_a2[:, :, tap].reshape(512, 512))
            if begun:
                dz[:, at] += part
            else:
                dz[:, at] = part
            begun = True
        pump()

    def plane_pairs(j):
        at = columns(j)
        pairs = []
        for plane in range(4):
            wide = columns(4 * plane + j)
            xhat = saved[HAT_A1][plane, :, at].astype(jnp.float32)
            v = xhat * par_mid[0:1, at] + par_mid[1:2, at]
            value = dz[:, wide] * slope(v)
            dz[:, wide] = value
            pairs.append((value, xhat))
        return pairs

    total = sums[SUM_A1]
    put_sums(plan, plane_pairs, mask, total.pay, 0, 512, pump)
    total.begin()
    flip[0:512] = dh_mid[...].T
    stages = total.stages()
    spatial_term(w_a2, saved[PATCH_A], 0, 3, 1)()
    stages[0]()
    spatial_term(w_a2, saved[PATCH_A], 3, 6, 1)()
    stages[1]()
    spatial_term(w_a2, saved[PATCH_A], 6, 9, 1)()
    pgrad_mid[0] = total.total[...]
    scale[0] = 0.25
    for plane in range(4):
        norm_back(
            lambda j, plane=plane: dz[:, columns(4 * plane + j)],
            saved[HAT_A1].at[plane],
            total.total,
            0,
            inv_mid.at[0],
            par_mid,
            0,
            planes[plane],
            4,
        )

    def input_gradient(p):
        target = (dh_a if p < 2 else dh_b).at[:, pl.ds((p % 2) * 1024, 1024)]
        value = dot(planes[p][...], w_a1[...].reshape(512, -1))
        if p == 0:
            value = value + saved[OUT_A][:, 0:1024].astype(jnp.float32)
            value = value + saved[OUT_A][:, 1024:2048].astype(jnp.float32)
        target[...] = value.astype(jnp.bfloat16)
        copy = pltpu.make_async_copy(target, dx_hbm.at[p], dx_sem.at[p])
        copy.start()
        return copy

    copies = []
    for p in range(4):
        copies.append(input_gradient(p))
        pump()

    def last_term(c, carry):
        at = quarter(c)
        total = jnp.zeros((512, 256), jnp.float32)
        for p in range(4):
            total = total + lax.dot_general(
                planes[p][...], x[p, :, at], (((0,), (0,)), ((), ())), preferred_element_type=jnp.float32
            )
        w_a1[:, :, 0, :, at] = total.astype(jnp.bfloat16).reshape(depth, 2, 64, 256)
        return carry

    paced(0, 4, last_term, 2, pump)
    reduce.enable(0)
    reduce.finish(weight_squares, squares_out)
    for copy in copies:
        copy.wait()
    for total in sums.values():
        total.close()


def run_backward(plan, depth, x, shifts, cot, mask, weight_squares, small, saved, fulls):
    rows, f32, bf16 = plan.rows, jnp.float32, jnp.bfloat16
    dma = pltpu.SemaphoreType.DMA
    scratch = []
    for _, pieces in backward_names(depth):
        scratch += pieces
    scratch += [pltpu.VMEM(value.shape, bf16) for value in (x, shifts, cot)]
    scratch += [pltpu.VMEM(full.shape, bf16) for full in fulls]
    scratch += [pltpu.VMEM(shape, kind) for name, (shape, kind) in zip(SAVED, saved_shapes(rows)) if name != PATCH_B]
    scratch += [
        pltpu.VMEM((rows, 2048), f32),
        pltpu.VMEM((rows, 512), f32),
        pltpu.VMEM((rows, 512), bf16),
        pltpu.VMEM((1024, rows), bf16),
        dma((10,)),
        dma((len(SAVED),)),
        dma((4,)),
    ]
    shapes = [full.shape for full in fulls]
    scratch += Reduce.scratch(shapes, depth)

    def part(shape, over):
        return jax.ShapeDtypeStruct((*shape[:3], shape[3] // over, shape[4]), bf16)

    outs = pl.pallas_call(
        functools.partial(backward_kernel, plan, depth),
        out_shape=[
            jax.ShapeDtypeStruct(x.shape, bf16),
            jax.ShapeDtypeStruct((4, 8, 512), f32),
            jax.ShapeDtypeStruct((8, 2048), f32),
            jax.ShapeDtypeStruct((8, 4096), f32),
            jax.ShapeDtypeStruct((8, 128), f32),
        ]
        + [jax.ShapeDtypeStruct(shape[2:], bf16) for shape in shapes]
        + [part(shape, 2) for shape in shapes]
        + [part(shape, 4) for shape in shapes],
        in_specs=[ANY] * 3 + [WHOLE] * 7 + [ANY] * len(SAVED) + [ANY] * 7,
        out_specs=[ANY] + [WHOLE] * 4 + [ANY] * 21,
        scratch_shapes=scratch,
        compiler_params=pltpu.CompilerParams(collective_id=1, has_side_effects=True, vmem_limit_bytes=VMEM_LIMIT),
    )(x, shifts, cot, mask, weight_squares, *small, *saved, *fulls)
    return outs[:12]


def scale_kernel(squares, *refs):
    totals, weights, outs, rest = refs[:7], refs[7:14], refs[14:28], refs[28:]
    totals_in, weights_in, staged = rest[:7], rest[7:14], rest[14:28]
    in_sem, out_sem = rest[28:]

    def loads(i):
        return (
            pltpu.make_async_copy(totals[i], totals_in[i], in_sem.at[0, i]),
            pltpu.make_async_copy(weights[i], weights_in[i], in_sem.at[1, i]),
        )

    def stores(i):
        return [pltpu.make_async_copy(staged[2 * i + n], outs[2 * i + n], out_sem.at[n, i]) for n in (0, 1)]

    for i in range(7):
        for copy in loads(i):
            copy.start()
    weight_norm = jnp.sqrt(squares[0:1, :])
    trust = weight_norm / (jnp.sqrt(squares[1:2, :]) + DECAY_RATE * weight_norm)
    for i in range(7):
        for copy in loads(i):
            copy.wait()
        ratio = trust[0:1, i : i + 1]

        def body(lead, carry, i=i, ratio=ratio):
            gradient = totals_in[i][lead].astype(jnp.float32)
            staged[2 * i][lead] = gradient
            decayed = gradient + DECAY_RATE * weights_in[i][lead].astype(jnp.float32)
            staged[2 * i + 1][lead] = ratio * decayed
            return carry

        lax.fori_loop(0, totals_in[i].shape[0], body, 0)
        for copy in stores(i):
            copy.start()
    for i in range(7):
        for copy in stores(i):
            copy.wait()


def run_scale(squares, totals, shards):
    f32, bf16, dma = jnp.float32, jnp.bfloat16, pltpu.SemaphoreType.DMA
    shapes = [total.shape for total in totals]
    outs = pl.pallas_call(
        scale_kernel,
        out_shape=[jax.ShapeDtypeStruct(shape, f32) for shape in shapes for _ in (0, 1)],
        in_specs=[WHOLE] + [ANY] * 14,
        out_specs=[ANY] * 14,
        scratch_shapes=[pltpu.VMEM(shape, bf16) for shape in shapes * 2]
        + [pltpu.VMEM(shape, f32) for shape in shapes for _ in (0, 1)]
        + [dma((2, 7)), dma((2, 7))],
        compiler_params=pltpu.CompilerParams(vmem_limit_bytes=VMEM_LIMIT),
    )(squares, *totals, *shards)
    return outs[0::2], outs[1::2]


def on_device(
    input_160,
    input_224,
    input_288,
    cotangent_160,
    cotangent_224,
    cotangent_288,
    live_counts,
    conv_a1,
    norm_a1,
    conv_a2,
    norm_a2,
    conv_a3,
    norm_a3,
    conv_as,
    norm_as,
    conv_b1,
    norm_b1,
    conv_b2,
    norm_b2,
    conv_b3,
    norm_b3,
):
    if conv_a1.shape[1] % 64 or conv_a3.shape[1] % 128 or lax.axis_size(REP) != 4:
        return plain_on_device(
            input_160,
            input_224,
            input_288,
            cotangent_160,
            cotangent_224,
            cotangent_288,
            live_counts,
            conv_a1,
            norm_a1,
            conv_a2,
            norm_a2,
            conv_a3,
            norm_a3,
            conv_as,
            norm_as,
            conv_b1,
            norm_b1,
            conv_b2,
            norm_b2,
            conv_b3,
            norm_b3,
        )
    depth = lax.axis_size(DP) // 2
    inputs = (input_160, input_224, input_288)
    plan = Plan([value.shape for value in inputs])
    shards = (
        conv_a1.T[None],
        jnp.transpose(conv_a2, (0, 1, 3, 2)).reshape(9, conv_a2.shape[3], conv_a2.shape[2]),
        conv_a3.reshape(2, -1, conv_a3.shape[1]),
        conv_as.reshape(4, -1, conv_as.shape[1]),
        conv_b1.T[None],
        jnp.transpose(conv_b2, (0, 1, 3, 2)).reshape(9, conv_b2.shape[3], conv_b2.shape[2]),
        conv_b3.reshape(2, -1, conv_b3.shape[1]),
    )

    planes, cotangents, masks, live_pixels = [], [], [], []
    for g, (value, cotangent) in enumerate(
        zip(inputs, (cotangent_160, cotangent_224, cotangent_288))
    ):
        side, slots, fill = plan.sides[g], plan.slots[g], plan.sizes[g] - plan.valid[g]
        split = jnp.transpose(value, (1, 2, 0, 3)).reshape(side, 2, side, 2, slots, -1)
        split = jnp.transpose(split, (1, 3, 0, 2, 4, 5)).reshape(4, plan.valid[g], -1)
        planes.append(jnp.pad(split, ((0, 0), (0, fill), (0, 0))))
        cotangents.append(
            jnp.pad(jnp.transpose(cotangent, (1, 2, 0, 3)).reshape(plan.valid[g], -1), ((0, fill), (0, 0)))
        )
        row = jnp.arange(plan.sizes[g])
        live = (lax.rem(row, slots) < live_counts[0, g]) & (row < plan.valid[g])
        masks.append(jnp.broadcast_to(live.astype(jnp.float32)[:, None], (plan.sizes[g], 128)))
        live_pixels.append((live_counts[0, g] * (side * side)).astype(jnp.float32))
    x = jnp.concatenate(planes, axis=1)
    cot = jnp.concatenate(cotangents, axis=0)
    mask = jnp.concatenate(masks, axis=0)
    counts = jnp.pad(jnp.stack(live_pixels), (0, 125)).reshape(1, 128)

    def stacked(norms):
        rows = jnp.concatenate(norms, axis=0).astype(jnp.float32)
        return jnp.pad(rows, ((0, 8 - rows.shape[0]), (0, 0)))

    mid_local, out_local = norm_a1.shape[1], norm_a3.shape[1]
    mid_width, out_width = mid_local * 2 * depth, out_local * 2 * depth
    norm_mid = lax.dynamic_update_slice(
        jnp.zeros((8, mid_width), jnp.float32),
        stacked((norm_a1, norm_a2, norm_b1, norm_b2)),
        (0, lax.axis_index(DP) * mid_local),
    )
    norm_out = stacked((norm_a3, norm_as, norm_b3))
    shifts = jnp.asarray(plan.shifts())

    out, *results = run_forward(plan, depth, x, shifts, mask, counts, norm_mid, norm_out, shards)
    small, square_row, fulls, saved = results[:5], results[5], results[6:13], results[13:]
    dx, pgrad_mid, pgrad_b3, pgrad_j, squares, *totals = run_backward(
        plan, depth, x, shifts, cot, mask, square_row, small, saved, fulls
    )

    def placed(values):
        return [
            values[0][0].T,
            jnp.transpose(values[1], (0, 2, 1)).reshape(conv_a2.shape),
            values[2].reshape(conv_a3.shape),
            values[3].reshape(conv_as.shape),
            values[4][0].T,
            jnp.transpose(values[5], (0, 2, 1)).reshape(conv_b2.shape),
            values[6].reshape(conv_b3.shape),
        ]

    gradients, scaled = run_scale(squares, totals, shards)
    gradients, scaled = placed(gradients), placed(scaled)

    def norm_gradient(sums, local):
        both = jnp.stack([sums[3] + sums[4] + sums[5], sums[0] + sums[1] + sums[2]])
        return lax.dynamic_slice_in_dim(both, lax.axis_index(DP) * local, local, 1)

    norm_gradients = (
        norm_gradient(pgrad_mid[0], mid_local),
        norm_gradient(pgrad_mid[1], mid_local),
        norm_gradient(pgrad_j[:, :out_width], out_local),
        norm_gradient(pgrad_j[:, out_width:], out_local),
        norm_gradient(pgrad_mid[2], mid_local),
        norm_gradient(pgrad_mid[3], mid_local),
        norm_gradient(pgrad_b3, out_local),
    )
    outputs, grad_inputs = [], []
    for g in range(3):
        side, slots, start = plan.sides[g], plan.slots[g], plan.starts[g]
        rows = out[start : start + plan.valid[g]].reshape(side, side, slots, -1)
        outputs.append(jnp.transpose(rows, (2, 0, 1, 3)))
        split = dx[:, start : start + plan.valid[g]].reshape(2, 2, side, side, slots, -1)
        split = jnp.transpose(split, (2, 0, 3, 1, 4, 5)).reshape(2 * side, 2 * side, slots, -1)
        grad_inputs.append(jnp.transpose(split, (2, 0, 1, 3)))
    pairs = [piece for pair in zip(gradients, norm_gradients) for piece in pair]
    return (*outputs, *grad_inputs, *pairs, *scaled, squares[0:2, 0:7])


def solution(mesh):
    by_image, by_column = P((DP, REP), None, None, None), P(None, DP)
    by_channel = P(None, None, None, DP)
    weights = [by_column, by_column, by_channel] + [by_column] * 7 + [by_channel] + [by_column] * 3
    kernels = [by_column, by_channel] + [by_column] * 3 + [by_channel, by_column]
    return jax.shard_map(
        on_device,
        mesh=mesh,
        in_specs=(*[by_image] * 6, P((DP, REP), None), *weights),
        out_specs=(*[by_image] * 6, *weights, *kernels, P()),
        check_vma=False,
    )
```

profile of v0, /device:TPU:0, one launch (start us, length us, event | category | flops | bytes accessed | tf_op | source)
XLA Modules:
  0.0 473.7 jit_solution(1203299242334107073)
XLA Ops:
  0.7 0.0 copy-start
  0.7 2.3 copy.74
  3.0 0.5 reshape.470
  3.5 0.0 copy-done
  3.6 0.8 copy.76
  4.4 0.3 reshape.468
  4.7 0.2 copy.63
  5.0 2.3 copy.75
  7.3 1.6 reshape.466
  8.9 0.0 copy-start.8
  9.0 0.0 copy-start.12
  9.0 0.0 copy-start.13
  9.0 0.0 copy-start.14
  9.0 0.0 copy-start.15
  9.0 0.0 copy-start.9
  9.0 0.0 copy-start.10
  9.0 0.0 copy-start.11
  9.0 1.9 fusion.5.refs_0_
  10.9 0.0 copy-done.8
  10.9 0.6 fusion.26
  11.5 0.6 and_convert_fusion
  12.1 1.3 and_convert_fusion.1
  13.4 0.1 maximum_maximum_fusion
  13.5 0.8 broadcast.68.refs_2_.refs_3_
  16.3 0.6 fusion.25.refs_3_
  16.9 0.0 copy-done.12
  16.9 0.0 copy-done.14
  16.9 0.3 dynamic_update_slice.3.refs_4_
  17.2 0.0 copy-start.5
  17.2 0.6 fusion.17.refs_5_
  17.8 197.5 %shard_map.429 = (bf16[384,2048]{1,0:T(8,128)(2,1)}, f32[4,8,512]{2,1,0:T(8,128)}, f32[3,8,2048]{2,1,0:T(8,128)}, f32[8,512]{1,0:T(8,128)}, f32[8,2048]{1,0:T(8,...) custom-call(bf16[4,384,1024]{2,1,0:T(8,128)(2,1)} %fusion.5.refs_0_,, ...), custom_call_target="tpu_custom_call" | custom-call | tf_op jit(solution)/shard_map/pallas_call | solution.py:1610
  215.3 1.0 slice.228
  216.3 0.9 reshape.477
  217.3 1.1 slice.229
  218.4 0.0 copy-start.3
  218.4 1.0 reshape.478
  219.4 1.2 slice.230
  220.6 1.3 reshape.479
  221.9 0.3 reshape.482
  222.2 0.2 reshape.481
  222.4 0.1 reshape.480
  222.5 1.3 fusion.11.refs_2_
  223.7 225.5 %shard_map.430 = (bf16[4,384,1024]{2,1,0:T(8,128)(2,1)}, f32[4,8,512]{2,1,0:T(8,128)}, f32[8,2048]{1,0:T(8,128)}, f32[8,4096]{1,0:T(8,128)}, f32[8,128]{1,0:T(8,...) custom-call(bf16[4,384,1024]{2,1,0:T(8,128)(2,1)} %fusion.5.refs_0_,, ...), custom_call_target="tpu_custom_call" | custom-call | tf_op jit(solution)/shard_map/pallas_call | solution.py:2015
  449.3 1.2 slice.231
  450.5 0.4 reshape.483
  450.9 1.4 copy.65
  452.2 1.2 slice.232
  453.4 0.6 reshape.499
  454.0 1.6 copy.67
  455.6 1.4 slice.233
  457.1 1.0 reshape.487
  458.0 2.3 copy.68
  460.3 7.0 %shard_map.431 = (f32[1,64,1024]{2,1,0:T(8,128)}, f32[1,64,1024]{2,1,0:T(8,128)}, f32[9,64,512]{2,1,0:T(8,128)}, f32[9,64,512]{2,1,0:T(8,128)}, f32[2,256,256]{2...) custom-call(f32[8,128]{1,0:T(8,128)} %get-tuple-element.107.squares,, ...), custom_call_target="tpu_custom_call" | custom-call | tf_op jit(solution)/shard_map/pallas_call | solution.py:2077
  467.3 0.0 copy-done.7
  467.4 0.6 fusion.24
  468.1 0.6 fusion.23
  468.7 0.0 copy-done.4
  468.7 0.1 slice_add_fusion.2
  468.8 0.7 fusion.20
  469.4 0.7 fusion.19
  470.1 0.6 fusion.22
  470.7 0.6 fusion.21
  471.4 0.7 fusion.18
  472.1 1.2 slice.276
  (20 shorter events, 0.1 us)
Async XLA Ops:
  0.7 2.9 copy-start
  8.9 2.0 copy-start.8
  9.0 7.9 %copy-start.12 = (bf16[2,64]{1,0:T(2,128)(2,1)S(1)}, bf16[2,64]{1,0:T(2,128)(2,1)}, u32[]{:S(2)}) copy-start(bf16[2,64]{1,0:T(2,128)(2,1)} %param.40) | copy-start | bytes 772
  9.0 7.9 %copy-start.13 = (bf16[2,64]{1,0:T(2,128)(2,1)S(1)}, bf16[2,64]{1,0:T(2,128)(2,1)}, u32[]{:S(2)}) copy-start(bf16[2,64]{1,0:T(2,128)(2,1)} %param.38) | copy-start | bytes 772
  9.0 7.9 %copy-start.14 = (bf16[2,64]{1,0:T(2,128)(2,1)S(1)}, bf16[2,64]{1,0:T(2,128)(2,1)}, u32[]{:S(2)}) copy-start(bf16[2,64]{1,0:T(2,128)(2,1)} %param.32) | copy-start | bytes 772
  9.0 7.9 %copy-start.15 = (bf16[2,64]{1,0:T(2,128)(2,1)S(1)}, bf16[2,64]{1,0:T(2,128)(2,1)}, u32[]{:S(2)}) copy-start(bf16[2,64]{1,0:T(2,128)(2,1)} %param.30) | copy-start | bytes 772
  9.0 8.2 %copy-start.9 = (bf16[2,256]{1,0:T(2,128)(2,1)S(1)}, bf16[2,256]{1,0:T(2,128)(2,1)}, u32[]{:S(2)}) copy-start(bf16[2,256]{1,0:T(2,128)(2,1)} %param.42) | copy-start | bytes 3076
  9.0 8.2 %copy-start.10 = (bf16[2,256]{1,0:T(2,128)(2,1)S(1)}, bf16[2,256]{1,0:T(2,128)(2,1)}, u32[]{:S(2)}) copy-start(bf16[2,256]{1,0:T(2,128)(2,1)} %param.36) | copy-start | bytes 3076
  9.0 8.2 %copy-start.11 = (bf16[2,256]{1,0:T(2,128)(2,1)S(1)}, bf16[2,256]{1,0:T(2,128)(2,1)}, u32[]{:S(2)}) copy-start(bf16[2,256]{1,0:T(2,128)(2,1)} %param.34) | copy-start | bytes 3076
  17.2 0.6 copy-start.5
  217.3 4.7 copy-start.1
  218.4 3.8 copy-start.3
  219.4 3.0 copy-start.2
  460.3 7.0 %copy-start.7 = (f32[4,8,512]{2,1,0:T(8,128)S(1)}, f32[4,8,512]{2,1,0:T(8,128)}, u32[]{:S(2)}) copy-start(f32[4,8,512]{2,1,0:T(8,128)} %get-tuple-element.116) | copy-start | bytes 196612
  460.3 8.4 %copy-start.4 = (f32[8,4096]{1,0:T(8,128)S(1)}, f32[8,4096]{1,0:T(8,128)}, u32[]{:S(2)}) copy-start(f32[8,4096]{1,0:T(8,128)} %get-tuple-element.119) | copy-start | bytes 393220
  460.3 11.0 %copy-start.6 = (f32[8,2048]{1,0:T(8,128)S(1)}, f32[8,2048]{1,0:T(8,128)}, u32[]{:S(2)}) copy-start(f32[8,2048]{1,0:T(8,128)} %get-tuple-element.124) | copy-start | bytes 196612
where the time goes:
time: 483 us; the launch traced here: 474 us
  Pallas kernels  430 us (89%)
  local copies, waits for them, and re-layouts  29.3 us (6%)
  other arithmetic  11 us (2%)
    pallas_call x1, Pallas kernels, run_backward(): pl.pallas_call(functools.partial(backward_kernel, plan, depth), out_shape...  226 us
    pallas_call x1, Pallas kernels, run_forward(): pl.pallas_call(functools.partial(forward_kernel, plan, depth), out_shape=...  197 us

commit v1 on v0

--- a/solution.py
+++ b/solution.py
@@ -474,7 +474,7 @@
 
 
 class Gather:
-    AHEAD = 2
+    AHEAD = 3
 
     def __init__(self, shards, fulls, sems, depth):
         self.shards, self.fulls, self.depth = shards, fulls, depth
@@ -601,26 +601,18 @@
 def taps(tensor):
     pieces = []
     for lead in (0, 3, 6):
-        pieces += [(tensor, lead, 1, True, column, 256) for column in (0, 256)]
-        pieces += [(tensor, lead + 1, 1, False, 0, 512), (tensor, lead + 2, 1, False, 0, 512)]
+        pieces += [(tensor, lead, 1, True, 0, 512), (tensor, lead + 1, 2, False, 0, 512)]
     return pieces
-
-
-def blocks(tensor, leads, both):
-    return [(tensor, lead, 1, lead in both, column, 128) for lead in leads for column in (0, 128)]
 
 
 CHUNKS = (
     [(0, 0, 1, False, column, 512) for column in (0, 512)],
     taps(1),
-    blocks(2, (0, 1), ()),
-    blocks(3, (0, 1, 2, 3), (0,)),
-    [
-        (4, 0, 1, width == 256, column, width)
-        for column, width in ((0, 256), (256, 256), (512, 512), (1024, 256), (1280, 256), (1536, 512))
-    ],
+    [(2, lead, 1, False, 0, 256) for lead in (0, 1)],
+    [(3, lead, 1, lead == 0, 0, 256) for lead in range(4)],
+    [(4, 0, 1, column % 1024 == 0, column, 512) for column in (0, 512, 1024, 1536)],
     taps(5),
-    blocks(6, (0, 1), ()),
+    [(6, lead, 1, False, 0, 256) for lead in (0, 1)],
 )
 GATHER_CHUNKS = [chunk for tensor in (0, 1, 3, 2, 4, 5, 6) for chunk in CHUNKS[tensor]]
 REDUCE_CHUNKS = [chunk for tensor in (6, 5, 4, 2, 3, 1, 0) for chunk in CHUNKS[tensor]]
@@ -681,8 +673,8 @@
             + [buffer(depth - 1, leads, part, columns) for leads, _, columns, part, _ in sizes]
             + [buffer(leads, part, columns) if both else buffer(16, 128) for leads, _, columns, part, both in sizes]
             + [buffer(leads, rows, columns) for leads, rows, columns, _, _ in sizes]
-            + [buffer(2, depth, 2, 1, shapes[2][3] // 2, 128), buffer(2, depth, 2, 1, shapes[0][3] // 2, 512)]
-            + [buffer(2, depth, 2, 1, shapes[2][3] // 4, 128), buffer(2, depth, 2, 1, shapes[0][3] // 4, 512)]
+            + [buffer(2, depth, 2, 1, shapes[2][3] // 2, shapes[2][4]), buffer(2, depth, 2, 2, shapes[0][3] // 2, 512)]
+            + [buffer(2, depth, 2, 1, shapes[2][3] // 4, shapes[2][4]), buffer(2, depth, 2, 2, shapes[0][3] // 4, 512)]
             + [pltpu.VMEM((2 * depth + 3, 8, 128), jnp.float32)]
             + [dma((2, count))] * 3
             + [dma((2, count, depth - 1)), dma((2, count)), dma((2, count, 3)), dma((2, depth)), dma((3, count))]
@@ -698,9 +690,9 @@
         return REDUCE_CHUNKS[k][2], REDUCE_CHUNKS[k][1]
 
     def slot(self, k, tall, wide):
-        tensor, columns = REDUCE_CHUNKS[k][0], REDUCE_CHUNKS[k][5]
+        tensor, _, leads = REDUCE_CHUNKS[k][:3]
         buffer = tall if tensor in (2, 3, 6) else wide
-        return buffer.at[k % 2, :, :, :, :, pl.ds(0, columns)]
+        return buffer.at[k % 2, :, :, pl.ds(0, leads)]
 
     def c_copy(self, k):
         held, rows, lead, cols, _ = self.piece(k)
@@ -1023,64 +1015,49 @@
 
 class Split:
     def __init__(self, refs, depth):
-        (self.pay, self.half, self.quad, self.deep, self.total, self.c_send, self.c_recv) = refs[:7]
-        (self.q_send, self.q_recv, self.z_send, self.z_recv, self.g_send, self.g_recv) = refs[7:]
+        (self.pay, self.near, self.deep, self.total, self.n_send, self.n_recv) = refs[:6]
+        (self.z_send, self.z_recv, self.g_send, self.g_recv) = refs[6:]
         self.depth = depth
         self.z, self.x, self.y, self.core = position()
         self.width = self.pay.shape[1]
-        self.mine = self.x * 2 + self.y
+        self.mine = self.x * 4 + self.y * 2 + self.core
 
     @staticmethod
     def scratch(width, depth):
         dma = pltpu.SemaphoreType.DMA
         return [
             pltpu.VMEM((8, width), jnp.float32),
-            pltpu.VMEM((8, width // 2), jnp.float32),
-            pltpu.VMEM((4, 8, width // 8), jnp.float32),
+            pltpu.VMEM((8, 8, width // 8), jnp.float32),
             pltpu.VMEM((depth, 8, width // 8), jnp.float32),
             pltpu.VMEM((8, width), jnp.float32),
-            dma((2,)),
-            dma((2,)),
-            dma((3,)),
-            dma((3,)),
+            dma((7,)),
+            dma((7,)),
             dma((depth - 1,)),
             dma((depth - 1,)),
-            dma((3,)),
-            dma((3,)),
+            dma((7,)),
+            dma((7,)),
         ]
 
-    def half_of(self, core):
-        return pl.ds(pl.multiple_of(core * (self.width // 2), 128), self.width // 2)
-
     def eighth_of(self, slot):
-        start = self.core * (self.width // 2) + slot * (self.width // 8)
-        return pl.ds(pl.multiple_of(start, 128), self.width // 8)
-
-    def core_copy(self):
-        return remote(
-            self.pay.at[:, self.half_of(1 - self.core)],
-            self.half,
-            self.c_send.at[0],
-            self.c_recv.at[0],
-            (self.z, self.x, self.y, 1 - self.core),
-        )
+        return pl.ds(pl.multiple_of(slot * (self.width // 8), 128), self.width // 8)
 
     def around(self):
-        for offset in range(1, 4):
-            x = 1 - self.x if offset & 2 else self.x
-            y = 1 - self.y if offset & 1 else self.y
-            yield offset - 1, x, y
-
-    def quad_copies(self):
+        for offset in range(1, 8):
+            x = 1 - self.x if offset & 4 else self.x
+            y = 1 - self.y if offset & 2 else self.y
+            core = 1 - self.core if offset & 1 else self.core
+            yield offset - 1, x, y, core
+
+    def near_copies(self):
         return [
             remote(
-                self.pay.at[:, self.eighth_of(x * 2 + y)],
-                self.quad.at[self.mine],
-                self.q_send.at[i],
-                self.q_recv.at[i],
-                (self.z, x, y, self.core),
+                self.pay.at[:, self.eighth_of(x * 4 + y * 2 + core)],
+                self.near.at[self.mine],
+                self.n_send.at[i],
+                self.n_recv.at[i],
+                (self.z, x, y, core),
             )
-            for i, x, y in self.around()
+            for i, x, y, core in self.around()
         ]
 
     def deep_copies(self):
@@ -1099,34 +1076,27 @@
     def gather_copies(self):
         here = self.total.at[:, self.eighth_of(self.mine)]
         return [
-            remote(here, here, self.g_send.at[i], self.g_recv.at[i], (self.z, x, y, self.core))
-            for i, x, y in self.around()
+            remote(here, here, self.g_send.at[i], self.g_recv.at[i], (self.z, x, y, core))
+            for i, x, y, core in self.around()
         ]
 
-    def last_copy(self):
-        here = self.total.at[:, self.half_of(self.core)]
-        return remote(here, here, self.c_send.at[1], self.c_recv.at[1], (self.z, self.x, self.y, 1 - self.core))
-
     def begin(self):
-        self.core_copy().start()
+        for copy in self.near_copies():
+            copy.start()
+        self.near[self.mine] = self.pay[:, self.eighth_of(self.mine)]
 
     def stages(self):
         def first():
-            self.core_copy().wait_recv()
-            half = self.half_of(self.core)
-            self.pay[:, half] = self.pay[:, half] + self.half[...]
-            for copy in self.quad_copies():
-                copy.start()
-            self.quad[self.mine] = self.pay[:, self.eighth_of(self.mine)]
-
-        def second():
-            for copy in self.quad_copies():
+            for copy in self.near_copies():
                 copy.wait_recv()
-            self.deep[self.z] = (self.quad[0] + self.quad[1]) + (self.quad[2] + self.quad[3])
+            total = self.near[0]
+            for slot in range(1, 8):
+                total = total + self.near[slot]
+            self.deep[self.z] = total
             for copy in self.deep_copies():
                 copy.start()
 
-        def third():
+        def second():
             for copy in self.deep_copies():
                 copy.wait_recv()
             total = self.deep[0]
@@ -1136,21 +1106,16 @@
             for copy in self.gather_copies():
                 copy.start()
 
-        def fourth():
+        def third():
             for copy in self.gather_copies():
                 copy.wait_recv()
-            self.last_copy().start()
-
-        def fifth():
-            self.last_copy().wait_recv()
-            for copy in self.gather_copies() + [self.last_copy()]:
+            for copy in self.gather_copies():
                 copy.wait_send()
 
-        return [first, second, third, fourth, fifth]
+        return [first, second, third]
 
     def close(self):
-        self.core_copy().wait_send()
-        for copy in self.quad_copies() + self.deep_copies():
+        for copy in self.near_copies() + self.deep_copies():
             copy.wait_send()
 
 
@@ -1165,7 +1130,7 @@
 
 
 HAT_A1, HAT_A2, HAT_A3, HAT_AS, HAT_B1, HAT_B2, HAT_B3, PATCH_A, PATCH_B, ACT_A2, ACT_B2, OUT_A = SAVED = range(12)
-SUM_A1, SUM_A2, SUM_A3, SUM_AS, SUM_B1, SUM_B2, SUM_B3, SUM_J = range(8)
+SUM_A1, SUM_A2, SUM_B1, SUM_B2, SUM_B3, SUM_J = range(6)
 
 
 def paced(first, last, body, parts, pump):
@@ -1209,6 +1174,12 @@
 
     def spans(self):
         return [slice(start, start + size) for start, size in zip(self.starts, self.sizes)]
+
+    def slot_rows(self):
+        out = np.full((self.rows, 128), 1e6, np.float32)
+        for start, valid, slots in zip(self.starts, self.valid, self.slots):
+            out[start : start + valid] = (np.arange(valid) % slots)[:, None]
+        return out
 
     def shifts(self):
         out = np.zeros((9, self.rows, self.rows), np.float32)
@@ -1241,16 +1212,16 @@
         paced(0, width // 128, body, 2, pump)
 
 
-def put_scales(total, inverse, over, width, factor=1.0):
+def put_scales(total, inverse, over, width, factor=1.0, base=0):
     def body(j, carry):
-        at = columns(j)
+        at, to = columns(base + j), columns(j)
         per = over[0:3, :] * factor
         means = total[0:3, at] * per
         variance = total[3:6, at] * per - means * means
         scales = lax.rsqrt(variance + EPSILON)
         zero = jnp.zeros((5, 128), jnp.float32)
         total[:, at] = jnp.concatenate([means, zero], axis=0)
-        inverse[:, at] = jnp.concatenate([scales, zero], axis=0)
+        inverse[:, to] = jnp.concatenate([scales, zero], axis=0)
         return carry
 
     lax.fori_loop(0, width // 128, body, 0)
@@ -1264,8 +1235,7 @@
     return (
         (SUM_A1, NearFar.scratch(512, depth)),
         (SUM_A2, NearFar.scratch(512, depth)),
-        (SUM_AS, Split.scratch(2048, depth)),
-        (SUM_A3, Split.scratch(2048, depth)),
+        (SUM_J, Split.scratch(4096, depth)),
         (SUM_B1, NearFar.scratch(512, depth)),
         (SUM_B2, NearFar.scratch(512, depth)),
         (SUM_B3, Split.scratch(2048, depth)),
@@ -1280,9 +1250,10 @@
         del refs[:count]
         return taken
 
-    x_hbm, shift_hbm, mask, counts, norm_mid, norm_out = take(6)
+    x_hbm, shift_hbm, slot_rows, live, norm_mid, norm_out = take(6)
     shards = take(7)
-    out, inv_mid, inv_out, par_mid, par_out, over, weight_squares = take(7)
+    outs = take(3)
+    mask, inv_mid, inv_out, par_mid, par_out, over, weight_squares = take(7)
     weights_hbm = take(7)
     saved_hbm = dict(zip(SAVED, take(len(SAVED))))
     sums = {}
@@ -1347,7 +1318,16 @@
     for copy in norm_copies(0) + norm_copies(1):
         copy.start()
     gather.begin()
-    rows = plan.rows
+    lanes = lax.broadcasted_iota(jnp.int32, (1, 128), 1)
+
+    def live_of(g):
+        return jnp.sum(jnp.where(lanes == g, live[...], 0.0), axis=1, keepdims=True)
+
+    for g, span in enumerate(plan.spans()):
+        mask[span, :] = jnp.where(slot_rows[span, :] < live_of(g), 1.0, 0.0)
+    counts = jnp.zeros((1, 128), jnp.float32)
+    for g, side in enumerate(plan.sides):
+        counts = counts + jnp.where(lanes == g, live[...] * float(side * side), 0.0)
 
     loads[0].wait()
     ready(0)
@@ -1356,20 +1336,18 @@
         hid_a1[p] = dot_nt(x[p], w_a1[...].reshape(512, -1))
         return carry
 
-    paced(0, 2, conv_a1, 2, pump)
-    paced(2, 4, conv_a1, 2, pump)
+    paced(0, 4, conv_a1, 2, pump)
 
     total = sums[SUM_A1]
     put_sums(
-        plan, lambda j: [(hid_a1[p, :, columns(j)],) * 2 for p in range(4)], mask, total.pay, 0, 512, pump
-    )
-    total.pay[6:7, 0:128] = counts[...]
+        plan, lambda j: [(hid_a1[p, :, columns(j)],) * 2 for p in range(4)], mask, total.pay, 0, 512
+    )
+    total.pay[6:7, 0:128] = counts
     total.begin()
     add_square(0)
+    total.stages()[0]()
+    total.stages()[1]()
     pump()
-    total.stages()[0]()
-    pump()
-    total.stages()[1]()
     for copy in norm_copies(0):
         copy.wait_recv()
     own_norms = norms_mid[0]
@@ -1378,7 +1356,6 @@
     par_mid[...] = own_norms
 
     pixels = total.total[6:7, 0:128]
-    lanes = lax.broadcasted_iota(jnp.int32, (1, 128), 1)
     inverse_counts = [
         jnp.broadcast_to(1.0 / jnp.sum(jnp.where(lanes == g, pixels, 0.0), axis=1, keepdims=True), (1, 128))
         for g in range(3)
@@ -1386,9 +1363,9 @@
     over[...] = jnp.concatenate(inverse_counts + [jnp.zeros((5, 128), jnp.float32)], axis=0)
     put_scales(total.total, inv_mid.at[0], over, 512, 0.25)
 
-    def normalized(hidden, total, inverse, hat, params, row, j):
-        at = columns(j)
-        xhat = by_group(plan, lambda g, span: (hidden[span] - total[g : g + 1, at]) * inverse[g : g + 1, at])
+    def normalized(hidden, total, inverse, hat, params, row, j, base=0):
+        at, sums_at = columns(j), columns(base + j)
+        xhat = by_group(plan, lambda g, span: (hidden[span] - total[g : g + 1, sums_at]) * inverse[g : g + 1, at])
         hat[:, at] = xhat.astype(jnp.bfloat16)
         return xhat * params[row : row + 1, at] + params[row + 1 : row + 2, at]
 
@@ -1412,7 +1389,7 @@
         )
         return carry
 
-    paced(0, 4, activate_a1, 4, pump)
+    paced(0, 4, activate_a1, 2, pump)
     save(HAT_A1)
 
     loads[1].wait()
@@ -1425,7 +1402,7 @@
             patch[tap] = act[plane]
         else:
             patch[tap] = dot(shift[matrix], act[plane]).astype(jnp.bfloat16)
-        if tap in (2, 5):
+        if tap == 4:
             pump()
     save(PATCH_A)
     ready(1)
@@ -1437,7 +1414,7 @@
             hid_mid[...] += dot_nt(patch[tap], weight[:, :, tap].reshape(512, 512))
             return carry
 
-        paced(1, 9, body, 3, pump)
+        paced(1, 9, body, 2, pump)
 
     spatial(patch, w_a2)
 
@@ -1449,10 +1426,7 @@
     def shortcut():
         ready(3)
         paced(0, 8, conv_as, 2, pump)
-        put_sums(plan, lambda j: [(hid_as[:, columns(j)],) * 2], mask, sums[SUM_AS].pay, 0, 2048, pump)
-        sums[SUM_AS].begin()
-
-    as_stages = sums[SUM_AS].stages()
+        put_sums(plan, lambda j: [(hid_as[:, columns(j)],) * 2], mask, sums[SUM_J].pay, 16, 2048)
 
     def mid_sums(total, name_index, works):
         put_sums(plan, lambda j: [(hid_mid[:, columns(j)],) * 2], mask, total.pay, 0, 512)
@@ -1460,7 +1434,8 @@
         interleave(total.stages(), works)
         put_scales(total.total, inv_mid.at[name_index], over, 512)
 
-    mid_sums(sums[SUM_A2], 1, [pump, lambda: add_square(1), pump])
+    mid_sums(sums[SUM_A2], 1, [lambda: add_square(1)])
+    pump()
     activate(
         lambda j: hid_mid[:, columns(j)], sums[SUM_A2].total, inv_mid.at[1], saved[HAT_A2], par_mid, 2, saved[ACT_A2]
     )
@@ -1475,39 +1450,36 @@
 
         paced(0, 8, body, 2, pump)
 
-    def out_sums(total, name_index, works):
-        put_sums(plan, lambda j: [(hid_out[:, columns(j)],) * 2], mask, total.pay, 0, 2048, pump)
-        total.begin()
-        interleave(total.stages(), works)
-        put_scales(total.total, inv_out.at[name_index], over, 2048)
-
     shortcut()
-    as_stages[0]()
+    pump()
     ready(2)
-    as_stages[1]()
     expand(saved[ACT_A2], w_a3)
-    as_stages[2]()
-    out_sums(sums[SUM_A3], 0, [as_stages[3], pump, as_stages[4], pump, lambda: add_square(2), lambda: add_square(3), pump])
-    put_scales(sums[SUM_AS].total, inv_out.at[1], over, 2048)
-
+    total = sums[SUM_J]
+    put_sums(plan, lambda j: [(hid_out[:, columns(j)],) * 2], mask, total.pay, 0, 2048)
+    total.begin()
+    interleave(total.stages(), [lambda: add_square(2), lambda: add_square(3)])
+    pump()
+    put_scales(total.total, inv_out.at[0], over, 2048)
+    put_scales(total.total, inv_out.at[1], over, 2048, base=16)
     for copy in norm_copies(1):
         copy.wait_recv()
     par_out[...] = norms_out[...]
 
     def join(j, carry):
         at = columns(j)
-        v = normalized(hid_out[:, at], sums[SUM_A3].total, inv_out.at[0], saved[HAT_A3], par_out, 0, j)
-        v = v + normalized(hid_as[:, at], sums[SUM_AS].total, inv_out.at[1], saved[HAT_AS], par_out, 2, j)
+        v = normalized(hid_out[:, at], total.total, inv_out.at[0], saved[HAT_A3], par_out, 0, j)
+        v = v + normalized(hid_as[:, at], total.total, inv_out.at[1], saved[HAT_AS], par_out, 2, j, 16)
         saved[OUT_A][:, at] = (v * sigmoid(v) * mask[...]).astype(jnp.bfloat16)
         return carry
 
-    paced(0, 16, join, 4, pump)
+    paced(0, 16, join, 3, pump)
     for name in (HAT_A3, HAT_AS, OUT_A):
         save(name)
 
     ready(4)
     hid_mid[...] = dot_nt(saved[OUT_A][...], w_b1[...].reshape(512, -1))
-    mid_sums(sums[SUM_B1], 2, [pump, lambda: add_square(4), pump])
+    mid_sums(sums[SUM_B1], 2, [lambda: add_square(4)])
+    pump()
     activate(
         lambda j: hid_mid[:, columns(j)], sums[SUM_B1].total, inv_mid.at[2], saved[HAT_B1], par_mid, 4, act.at[0]
     )
@@ -1517,11 +1489,12 @@
         saved[PATCH_B][tap] = dot(shift[tap], act[0]).astype(jnp.bfloat16)
         return carry
 
-    paced(0, 9, patches, 3, pump)
+    paced(0, 9, patches, 2, pump)
     save(PATCH_B)
     ready(5)
     spatial(saved[PATCH_B], w_b2)
-    mid_sums(sums[SUM_B2], 3, [pump, lambda: add_square(5), pump])
+    mid_sums(sums[SUM_B2], 3, [lambda: add_square(5)])
+    pump()
     activate(
         lambda j: hid_mid[:, columns(j)], sums[SUM_B2].total, inv_mid.at[3], saved[HAT_B2], par_mid, 6, saved[ACT_B2]
     )
@@ -1529,13 +1502,20 @@
     save(ACT_B2)
     ready(6)
     expand(saved[ACT_B2], w_b3)
-    out_sums(sums[SUM_B3], 2, [lambda: add_square(6)])
+    total_b = sums[SUM_B3]
+    put_sums(plan, lambda j: [(hid_out[:, columns(j)],) * 2], mask, total_b.pay, 0, 2048)
+    total_b.begin()
+    interleave(total_b.stages(), [lambda: add_square(6)])
+    put_scales(total_b.total, inv_out.at[2], over, 2048)
 
     def finish(j, carry):
         at = columns(j)
-        v = normalized(hid_out[:, at], sums[SUM_B3].total, inv_out.at[2], saved[HAT_B3], par_out, 4, j)
+        v = normalized(hid_out[:, at], total_b.total, inv_out.at[2], saved[HAT_B3], par_out, 4, j)
         v = v + saved[OUT_A][:, at].astype(jnp.float32)
-        out[:, at] = (v * sigmoid(v) * mask[...]).astype(jnp.bfloat16)
+        v = v * sigmoid(v) * mask[...]
+        for g, target in enumerate(outs):
+            start = plan.starts[g]
+            target[:, at] = v[start : start + plan.valid[g]].astype(jnp.bfloat16)
         return carry
 
     lax.fori_loop(0, 16, finish, 0)
@@ -1573,7 +1553,7 @@
 VMEM_LIMIT = 62 * 1024 * 1024
 
 
-def run_forward(plan, depth, x, shifts, mask, counts, norm_mid, norm_out, shards):
+def run_forward(plan, depth, x, shifts, slot_rows, live, norm_mid, norm_out, shards):
     rows, f32, bf16 = plan.rows, jnp.float32, jnp.bfloat16
     dma = pltpu.SemaphoreType.DMA
     scratch = []
@@ -1598,8 +1578,9 @@
         dma((2, 2 * depth)),
     ]
     scratch += Gather.scratch(depth)
-    small = [
-        jax.ShapeDtypeStruct((rows, 2048), bf16),
+    small = [jax.ShapeDtypeStruct((valid, 2048), bf16) for valid in plan.valid]
+    small += [
+        jax.ShapeDtypeStruct((rows, 128), f32),
         jax.ShapeDtypeStruct((4, 8, 512), f32),
         jax.ShapeDtypeStruct((3, 8, 2048), f32),
         jax.ShapeDtypeStruct((8, 512), f32),
@@ -1611,10 +1592,10 @@
         functools.partial(forward_kernel, plan, depth),
         out_shape=small + fulls + [jax.ShapeDtypeStruct(shape, kind) for shape, kind in saved_shapes(rows)],
         in_specs=[ANY, ANY] + [WHOLE] * 4 + [ANY] * 7,
-        out_specs=[WHOLE] * 7 + [ANY] * 7 + [ANY] * len(SAVED),
+        out_specs=[WHOLE] * 10 + [ANY] * 7 + [ANY] * len(SAVED),
         scratch_shapes=scratch,
         compiler_params=pltpu.CompilerParams(collective_id=0, has_side_effects=True, vmem_limit_bytes=VMEM_LIMIT),
-    )(x, shifts, mask, counts, norm_mid, norm_out, *shards)
+    )(x, shifts, slot_rows, live, norm_mid, norm_out, *shards)
 
 
 def backward_names(depth):
@@ -1741,7 +1722,7 @@
             dact[...] += dot_nt(dh[:, quarter(d)], weight[d // 2, lax.rem(d, 2)].reshape(512, 256))
             return carry
 
-        paced(1, 8, body, 2, pump)
+        lax.fori_loop(1, 8, body, 0)
 
     def expand_term(lhs, dh, weight, first_slot, last_slot):
         def body(d, carry):
@@ -1762,24 +1743,18 @@
 
     def mid_norm(name, hat, index, row, works):
         total = sums[name]
-        put_sums(plan, mid_pairs(hat, row), mask, total.pay, 0, 512, pump)
+        put_sums(plan, mid_pairs(hat, row), mask, total.pay, 0, 512)
         total.begin()
         interleave(total.stages(), works)
         pgrad_mid[index] = total.total[...]
         norm_back(lambda j: dact[:, columns(j)], saved[hat], total.total, 0, inv_mid.at[index], par_mid, row, dh_mid, 4)
 
     contract(dh_a, w_b3)
-
-    def third_term(part):
-        def work():
-            expand_term(flip[0:512, :], dh_a, w_b3, 4 * part, 4 * part + 4)
-            if part:
-                reduce.enable(6)
-                pump()
-
-        return work
-
-    mid_norm(SUM_B2, HAT_B2, 3, 6, [third_term(0), third_term(1)])
+    expand_term(flip[0:512, :], dh_a, w_b3, 0, 8)
+    reduce.enable(6)
+    pump()
+    mid_norm(SUM_B2, HAT_B2, 3, 6, [])
+    pump()
 
     def spread(tap, carry):
         part = dot(
@@ -1788,7 +1763,7 @@
         dact[...] = part + jnp.where(tap == 0, 0.0, dact[...])
         return carry
 
-    paced(0, 9, spread, 5, pump)
+    paced(0, 9, spread, 2, pump)
     flip[0:512] = dh_mid[...].T
 
     def spatial_term(weight, patch, first_tap, last_tap, tensor):
@@ -1799,7 +1774,6 @@
 
             lax.fori_loop(first_tap, last_tap, body, 0)
             reduce.enable(tensor, last_tap)
-            pump()
 
         return work
 
@@ -1810,7 +1784,9 @@
         4,
         [spatial_term(w_b2, saved[PATCH_B], 0, 3, 5), spatial_term(w_b2, saved[PATCH_B], 3, 6, 5)],
     )
+    pump()
     spatial_term(w_b2, saved[PATCH_B], 6, 9, 5)()
+    pump()
     loading(PATCH_A).start()
 
     def residual(d, carry):
@@ -1832,7 +1808,7 @@
     total = sums[SUM_J]
     put_sums(plan, join_pairs, mask, total.pay, 0, 2048, pump)
     put_sums(
-        plan, lambda j: [(dz[:, columns(j)], saved[HAT_AS][:, columns(j)].astype(jnp.float32))], mask, total.pay, 16, 2048, pump
+        plan, lambda j: [(dz[:, columns(j)], saved[HAT_AS][:, columns(j)].astype(jnp.float32))], mask, total.pay, 16, 2048
     )
     total.begin()
     flip[0:512] = dh_mid[...].T
@@ -1848,7 +1824,6 @@
             lax.fori_loop(2 * part, 2 * part + 2, body, 0)
             if part == 3:
                 reduce.enable(4)
-            pump()
 
         return work
 
@@ -1866,11 +1841,8 @@
     flip[0:512] = saved[ACT_A2][...].T
 
     def third_term_a():
-        expand_term(flip[0:512, :], dh_a, w_a3, 0, 4)
-        pump()
-        expand_term(flip[0:512, :], dh_a, w_a3, 4, 8)
+        expand_term(flip[0:512, :], dh_a, w_a3, 0, 8)
         reduce.enable(2)
-        pump()
 
     def shortcut():
         even = dz.at[:, 0:1024]
@@ -1880,7 +1852,7 @@
             even[...] += dot_nt(dh_b[:, quarter(d)], w_as[d // 2, lax.rem(d, 2)].reshape(1024, 256))
             return carry
 
-        paced(1, 8, body, 3, pump)
+        lax.fori_loop(1, 8, body, 0)
 
         def keep(j, carry):
             value = even[:, columns(j)]
@@ -1902,6 +1874,8 @@
     for plane in range(4):
         at = slice(plane * 512, plane * 512 + 512)
         begun = False
+        if plane == 2:
+            pump()
         for tap in range(9):
             a, b = tap // 3, tap % 3
             if plane != (0 if a == 1 else 2) + (0 if b == 1 else 1):
@@ -1914,7 +1888,7 @@
             else:
                 dz[:, at] = part
             begun = True
-        pump()
+    pump()
 
     def plane_pairs(j):
         at = columns(j)
@@ -1929,7 +1903,7 @@
         return pairs
 
     total = sums[SUM_A1]
-    put_sums(plan, plane_pairs, mask, total.pay, 0, 512, pump)
+    put_sums(plan, plane_pairs, mask, total.pay, 0, 512)
     total.begin()
     flip[0:512] = dh_mid[...].T
     stages = total.stages()
@@ -1937,7 +1911,9 @@
     stages[0]()
     spatial_term(w_a2, saved[PATCH_A], 3, 6, 1)()
     stages[1]()
+    pump()
     spatial_term(w_a2, saved[PATCH_A], 6, 9, 1)()
+    pump()
     pgrad_mid[0] = total.total[...]
     scale[0] = 0.25
     for plane in range(4):
@@ -2032,10 +2008,17 @@
     return outs[:12]
 
 
-def scale_kernel(squares, *refs):
-    totals, weights, outs, rest = refs[:7], refs[7:14], refs[14:28], refs[28:]
-    totals_in, weights_in, staged = rest[:7], rest[7:14], rest[14:28]
-    in_sem, out_sem = rest[28:]
+def scale_kernel(depth, squares, sums_mid, sums_b3, sums_j, *refs):
+    refs = list(refs)
+
+    def take(count):
+        taken = refs[:count]
+        del refs[:count]
+        return taken
+
+    totals, weights, outs, norm_outs = take(7), take(7), take(14), take(7)
+    squares_out, totals_in, weights_in, staged = take(1)[0], take(7), take(7), take(14)
+    in_sem, out_sem = refs
 
     def loads(i):
         return (
@@ -2049,6 +2032,39 @@
     for i in range(7):
         for copy in loads(i):
             copy.start()
+
+    squares_out[...] = squares[0:2, 0:7]
+    place = lax.axis_index(DP)
+
+    def both(sums):
+        seconds = sums[3:4] + sums[4:5] + sums[5:6]
+        return jnp.concatenate([seconds, sums[0:1] + sums[1:2] + sums[2:3]], axis=0)
+
+    def put(target, sums, base):
+        width = target.shape[1]
+        span = max(width, 128)
+        start = (place * width) // span * span + base
+        block = both(sums[:, pl.ds(pl.multiple_of(start, 128), span)])
+        for piece in range(span // width):
+            part = block[:, piece * width : (piece + 1) * width]
+
+            @pl.when(lax.rem(place, span // width) == piece)
+            def _(part=part):
+                target[...] = part
+
+    for i, (sums, base) in enumerate(
+        (
+            (sums_mid.at[0], 0),
+            (sums_mid.at[1], 0),
+            (sums_j, 0),
+            (sums_j, sums_j.shape[1] // 2),
+            (sums_mid.at[2], 0),
+            (sums_mid.at[3], 0),
+            (sums_b3, 0),
+        )
+    ):
+        put(norm_outs[i], sums, base)
+
     weight_norm = jnp.sqrt(squares[0:1, :])
     trust = weight_norm / (jnp.sqrt(squares[1:2, :]) + DECAY_RATE * weight_norm)
     for i in range(7):
@@ -2071,20 +2087,22 @@
             copy.wait()
 
 
-def run_scale(squares, totals, shards):
+def run_scale(depth, squares, sums, totals, shards, widths):
     f32, bf16, dma = jnp.float32, jnp.bfloat16, pltpu.SemaphoreType.DMA
     shapes = [total.shape for total in totals]
     outs = pl.pallas_call(
-        scale_kernel,
-        out_shape=[jax.ShapeDtypeStruct(shape, f32) for shape in shapes for _ in (0, 1)],
-        in_specs=[WHOLE] + [ANY] * 14,
-        out_specs=[ANY] * 14,
+        functools.partial(scale_kernel, depth),
+        out_shape=[jax.ShapeDtypeStruct(shape, f32) for shape in shapes for _ in (0, 1)]
+        + [jax.ShapeDtypeStruct((2, width), f32) for width in widths]
+        + [jax.ShapeDtypeStruct((2, 7), f32)],
+        in_specs=[WHOLE] * 4 + [ANY] * 14,
+        out_specs=[ANY] * 14 + [WHOLE] * 8,
         scratch_shapes=[pltpu.VMEM(shape, bf16) for shape in shapes * 2]
         + [pltpu.VMEM(shape, f32) for shape in shapes for _ in (0, 1)]
         + [dma((2, 7)), dma((2, 7))],
         compiler_params=pltpu.CompilerParams(vmem_limit_bytes=VMEM_LIMIT),
-    )(squares, *totals, *shards)
-    return outs[0::2], outs[1::2]
+    )(squares, *sums, *totals, *shards)
+    return outs[0:14:2], outs[1:14:2], outs[14:21], outs[21]
 
 
 def on_device(
@@ -2147,7 +2165,7 @@
         conv_b3.reshape(2, -1, conv_b3.shape[1]),
     )
 
-    planes, cotangents, masks, live_pixels = [], [], [], []
+    planes, cotangents = [], []
     for g, (value, cotangent) in enumerate(
         zip(inputs, (cotangent_160, cotangent_224, cotangent_288))
     ):
@@ -2158,21 +2176,16 @@
         cotangents.append(
             jnp.pad(jnp.transpose(cotangent, (1, 2, 0, 3)).reshape(plan.valid[g], -1), ((0, fill), (0, 0)))
         )
-        row = jnp.arange(plan.sizes[g])
-        live = (lax.rem(row, slots) < live_counts[0, g]) & (row < plan.valid[g])
-        masks.append(jnp.broadcast_to(live.astype(jnp.float32)[:, None], (plan.sizes[g], 128)))
-        live_pixels.append((live_counts[0, g] * (side * side)).astype(jnp.float32))
     x = jnp.concatenate(planes, axis=1)
     cot = jnp.concatenate(cotangents, axis=0)
-    mask = jnp.concatenate(masks, axis=0)
-    counts = jnp.pad(jnp.stack(live_pixels), (0, 125)).reshape(1, 128)
+    live = jnp.pad(live_counts.astype(jnp.float32), ((0, 0), (0, 128 - live_counts.shape[1])))
 
     def stacked(norms):
         rows = jnp.concatenate(norms, axis=0).astype(jnp.float32)
         return jnp.pad(rows, ((0, 8 - rows.shape[0]), (0, 0)))
 
-    mid_local, out_local = norm_a1.shape[1], norm_a3.shape[1]
-    mid_width, out_width = mid_local * 2 * depth, out_local * 2 * depth
+    mid_local = norm_a1.shape[1]
+    mid_width = mid_local * 2 * depth
     norm_mid = lax.dynamic_update_slice(
         jnp.zeros((8, mid_width), jnp.float32),
         stacked((norm_a1, norm_a2, norm_b1, norm_b2)),
@@ -2181,8 +2194,11 @@
     norm_out = stacked((norm_a3, norm_as, norm_b3))
     shifts = jnp.asarray(plan.shifts())
 
-    out, *results = run_forward(plan, depth, x, shifts, mask, counts, norm_mid, norm_out, shards)
-    small, square_row, fulls, saved = results[:5], results[5], results[6:13], results[13:]
+    results = run_forward(
+        plan, depth, x, shifts, jnp.asarray(plan.slot_rows()), live, norm_mid, norm_out, shards
+    )
+    outs, mask, small, square_row = results[:3], results[3], results[4:9], results[9]
+    fulls, saved = results[10:17], results[17:]
     dx, pgrad_mid, pgrad_b3, pgrad_j, squares, *totals = run_backward(
         plan, depth, x, shifts, cot, mask, square_row, small, saved, fulls
     )
@@ -2198,32 +2214,22 @@
             values[6].reshape(conv_b3.shape),
         ]
 
-    gradients, scaled = run_scale(squares, totals, shards)
+    widths = [norm.shape[1] for norm in (norm_a1, norm_a2, norm_a3, norm_as, norm_b1, norm_b2, norm_b3)]
+    gradients, scaled, norm_gradients, squares = run_scale(
+        depth, squares, (pgrad_mid, pgrad_b3, pgrad_j), totals, shards, widths
+    )
     gradients, scaled = placed(gradients), placed(scaled)
 
-    def norm_gradient(sums, local):
-        both = jnp.stack([sums[3] + sums[4] + sums[5], sums[0] + sums[1] + sums[2]])
-        return lax.dynamic_slice_in_dim(both, lax.axis_index(DP) * local, local, 1)
-
-    norm_gradients = (
-        norm_gradient(pgrad_mid[0], mid_local),
-        norm_gradient(pgrad_mid[1], mid_local),
-        norm_gradient(pgrad_j[:, :out_width], out_local),
-        norm_gradient(pgrad_j[:, out_width:], out_local),
-        norm_gradient(pgrad_mid[2], mid_local),
-        norm_gradient(pgrad_mid[3], mid_local),
-        norm_gradient(pgrad_b3, out_local),
-    )
     outputs, grad_inputs = [], []
     for g in range(3):
         side, slots, start = plan.sides[g], plan.slots[g], plan.starts[g]
-        rows = out[start : start + plan.valid[g]].reshape(side, side, slots, -1)
+        rows = outs[g].reshape(side, side, slots, -1)
         outputs.append(jnp.transpose(rows, (2, 0, 1, 3)))
         split = dx[:, start : start + plan.valid[g]].reshape(2, 2, side, side, slots, -1)
         split = jnp.transpose(split, (2, 0, 3, 1, 4, 5)).reshape(2 * side, 2 * side, slots, -1)
         grad_inputs.append(jnp.transpose(split, (2, 0, 1, 3)))
     pairs = [piece for pair in zip(gradients, norm_gradients) for piece in pair]
-    return (*outputs, *grad_inputs, *pairs, *scaled, squares[0:2, 0:7])
+    return (*outputs, *grad_inputs, *pairs, *scaled, squares)
 
 
 def solution(mesh):

time: 483 us -> 466 us (0.965)
  Pallas kernels: 430 us -> 420 us
    pallas_call x1, Pallas kernels: 197 us -> 190 us  [run_forward(): pl.pallas_call(functools.partial(forward_kernel, plan, depth), out_shape=...]
    slice x5 -> x0, local copies, waits for them, and re-layouts: 5.15 us -> none  [the longest x3 3.33 us: on_device(): rows = out[start:start + plan.valid[g]].reshape(side, side, slots, -1)]
where the time goes in v1:
time: 466 us; the launch traced here: 456 us
  Pallas kernels  420 us (90%)
  local copies, waits for them, and re-layouts  28.3 us (6%)
  other arithmetic  6.79 us (1%)
    pallas_call x1, Pallas kernels, run_backward(): pl.pallas_call(functools.partial(backward_kernel, plan, depth), out_shape...  223 us
    pallas_call x1, Pallas kernels, run_forward(): pl.pallas_call(functools.partial(forward_kernel, plan, depth), out_shape=...  190 us

profile of v1, /device:TPU:0, one launch (start us, length us, event | category | flops | bytes accessed | tf_op | source)
XLA Modules:
  0.0 456.5 jit_solution(2279813771854697329)
XLA Ops:
  0.7 0.7 convert_element_type.23
  1.3 0.5 pad.37.refs_3_
  1.8 0.7 maximum_convert_fusion
  2.6 1.3 fusion.17.refs_5_
  3.9 0.1 dynamic_update_slice.3.refs_4_
  4.0 0.0 copy-start.2
  4.0 1.1 reshape.169
  5.1 0.0 copy-done.2
  5.1 0.0 copy-start.1
  5.2 1.2 reshape.170
  6.4 2.1 reshape.171
  8.5 1.2 fusion.11.refs_2_
  9.7 0.0 copy-done.1
  9.7 0.0 copy-start
  9.7 0.8 copy.77
  10.6 0.3 reshape.158
  10.9 0.2 copy.64
  11.2 0.0 copy-done
  11.2 0.3 copy.76
  11.5 1.1 reshape.156
  12.6 2.2 copy.75
  14.8 0.5 reshape.160
  15.4 2.9 fusion.5.refs_0_
  18.2 189.9 %shard_map.438 = (bf16[100,2048]{1,0:T(8,128)(2,1)}, bf16[98,2048]{1,0:T(8,128)(2,1)}, bf16[162,2048]{1,0:T(8,128)(2,1)}, f32[384,128]{1,0:T(8,128)}, f32[4,8,51...) custom-call(bf16[4,384,1024]{2,1,0:T(8,128)(2,1)} %fusion.5.refs_0_,, ...), custom_call_target="tpu_custom_call" | custom-call | tf_op jit(solution)/shard_map/pallas_call | solution.py:1591
  208.1 1.9 reshape.166
  210.1 2.0 reshape.167
  212.1 2.6 reshape.168
  214.7 222.6 %shard_map.439 = (bf16[4,384,1024]{2,1,0:T(8,128)(2,1)}, f32[4,8,512]{2,1,0:T(8,128)}, f32[8,2048]{1,0:T(8,128)}, f32[8,4096]{1,0:T(8,128)}, f32[8,128]{1,0:T(8,...) custom-call(bf16[4,384,1024]{2,1,0:T(8,128)(2,1)} %fusion.5.refs_0_,, ...), custom_call_target="tpu_custom_call" | custom-call | tf_op jit(solution)/shard_map/pallas_call | solution.py:1991
  437.3 1.2 slice.10
  438.5 0.6 reshape.188
  439.1 1.6 copy.68
  440.7 1.2 slice.9
  441.9 1.4 slice.11
  443.4 1.0 reshape.176
  444.3 0.4 reshape.172
  444.7 1.4 copy.66
  446.1 2.3 copy.69
  448.4 7.9 %shard_map.440 = (f32[1,64,1024]{2,1,0:T(8,128)}, f32[1,64,1024]{2,1,0:T(8,128)}, f32[9,64,512]{2,1,0:T(8,128)}, f32[9,64,512]{2,1,0:T(8,128)}, f32[2,256,256]{2...) custom-call(f32[8,128]{1,0:T(8,128)} %get-tuple-element.121.squares,, ...), custom_call_target="tpu_custom_call" | custom-call | tf_op jit(solution)/shard_map/pallas_call | solution.py:2093
  (1 shorter events, 0.0 us)
Async XLA Ops:
  4.0 1.1 copy-start.2
  5.1 4.6 %copy-start.1 = (bf16[2,14,14,1024]{3,0,2,1:T(2,128)(2,1)S(1)}, bf16[2,14,14,1024]{3,0,2,1:T(2,128)(2,1)}, u32[]{:S(2)}) copy-start(bf16[2,14,14,1024]{3,0,2,1:T(2,128)(2,1)} %param.24) | copy-start | bytes 2408452
  9.7 1.4 copy-start

commit v2 on v1

--- a/solution.py
+++ b/solution.py
@@ -1336,7 +1336,9 @@
         hid_a1[p] = dot_nt(x[p], w_a1[...].reshape(512, -1))
         return carry
 
-    paced(0, 4, conv_a1, 2, pump)
+    lax.fori_loop(0, 2, conv_a1, 0)
+    pump()
+    lax.fori_loop(2, 4, conv_a1, 0)
 
     total = sums[SUM_A1]
     put_sums(
@@ -1345,9 +1347,10 @@
     total.pay[6:7, 0:128] = counts
     total.begin()
     add_square(0)
+    pump()
     total.stages()[0]()
+    pump()
     total.stages()[1]()
-    pump()
     for copy in norm_copies(0):
         copy.wait_recv()
     own_norms = norms_mid[0]
@@ -1389,7 +1392,9 @@
         )
         return carry
 
-    paced(0, 4, activate_a1, 2, pump)
+    lax.fori_loop(0, 2, activate_a1, 0)
+    pump()
+    lax.fori_loop(2, 4, activate_a1, 0)
     save(HAT_A1)
 
     loads[1].wait()
@@ -1414,7 +1419,7 @@
             hid_mid[...] += dot_nt(patch[tap], weight[:, :, tap].reshape(512, 512))
             return carry
 
-        paced(1, 9, body, 2, pump)
+        lax.fori_loop(1, 9, body, 0)
 
     spatial(patch, w_a2)
 
@@ -1425,7 +1430,7 @@
 
     def shortcut():
         ready(3)
-        paced(0, 8, conv_as, 2, pump)
+        lax.fori_loop(0, 8, conv_as, 0)
         put_sums(plan, lambda j: [(hid_as[:, columns(j)],) * 2], mask, sums[SUM_J].pay, 16, 2048)
 
     def mid_sums(total, name_index, works):
@@ -1434,8 +1439,7 @@
         interleave(total.stages(), works)
         put_scales(total.total, inv_mid.at[name_index], over, 512)
 
-    mid_sums(sums[SUM_A2], 1, [lambda: add_square(1)])
-    pump()
+    mid_sums(sums[SUM_A2], 1, [pump, lambda: add_square(1), pump])
     activate(
         lambda j: hid_mid[:, columns(j)], sums[SUM_A2].total, inv_mid.at[1], saved[HAT_A2], par_mid, 2, saved[ACT_A2]
     )
@@ -1448,17 +1452,15 @@
             hid_out[:, at] = dot(act_ref[...], weight[d // 2, lax.rem(d, 2)].reshape(512, 256))
             return carry
 
-        paced(0, 8, body, 2, pump)
+        lax.fori_loop(0, 8, body, 0)
 
     shortcut()
-    pump()
     ready(2)
     expand(saved[ACT_A2], w_a3)
     total = sums[SUM_J]
     put_sums(plan, lambda j: [(hid_out[:, columns(j)],) * 2], mask, total.pay, 0, 2048)
     total.begin()
-    interleave(total.stages(), [lambda: add_square(2), lambda: add_square(3)])
-    pump()
+    interleave(total.stages(), [pump, lambda: add_square(2), pump, lambda: add_square(3), pump])
     put_scales(total.total, inv_out.at[0], over, 2048)
     put_scales(total.total, inv_out.at[1], over, 2048, base=16)
     for copy in norm_copies(1):
@@ -1472,14 +1474,13 @@
         saved[OUT_A][:, at] = (v * sigmoid(v) * mask[...]).astype(jnp.bfloat16)
         return carry
 
-    paced(0, 16, join, 3, pump)
+    lax.fori_loop(0, 16, join, 0)
     for name in (HAT_A3, HAT_AS, OUT_A):
         save(name)
 
     ready(4)
     hid_mid[...] = dot_nt(saved[OUT_A][...], w_b1[...].reshape(512, -1))
-    mid_sums(sums[SUM_B1], 2, [lambda: add_square(4)])
-    pump()
+    mid_sums(sums[SUM_B1], 2, [pump, lambda: add_square(4), pump])
     activate(
         lambda j: hid_mid[:, columns(j)], sums[SUM_B1].total, inv_mid.at[2], saved[HAT_B1], par_mid, 4, act.at[0]
     )
@@ -1489,12 +1490,11 @@
         saved[PATCH_B][tap] = dot(shift[tap], act[0]).astype(jnp.bfloat16)
         return carry
 
-    paced(0, 9, patches, 2, pump)
+    lax.fori_loop(0, 9, patches, 0)
     save(PATCH_B)
     ready(5)
     spatial(saved[PATCH_B], w_b2)
-    mid_sums(sums[SUM_B2], 3, [lambda: add_square(5)])
-    pump()
+    mid_sums(sums[SUM_B2], 3, [pump, lambda: add_square(5), pump])
     activate(
         lambda j: hid_mid[:, columns(j)], sums[SUM_B2].total, inv_mid.at[3], saved[HAT_B2], par_mid, 6, saved[ACT_B2]
     )
@@ -1685,7 +1685,7 @@
             target[:, at] = (by_group(plan, of) * mask[...]).astype(jnp.bfloat16)
             return carry
 
-        paced(0, blocks, body, 1 if blocks == 4 else 2, pump)
+        lax.fori_loop(0, blocks, body, 0)
 
     scale = [1.0]
 
@@ -1753,8 +1753,7 @@
     expand_term(flip[0:512, :], dh_a, w_b3, 0, 8)
     reduce.enable(6)
     pump()
-    mid_norm(SUM_B2, HAT_B2, 3, 6, [])
-    pump()
+    mid_norm(SUM_B2, HAT_B2, 3, 6, [pump, pump])
 
     def spread(tap, carry):
         part = dot(
@@ -1763,7 +1762,7 @@
         dact[...] = part + jnp.where(tap == 0, 0.0, dact[...])
         return carry
 
-    paced(0, 9, spread, 2, pump)
+    lax.fori_loop(0, 9, spread, 0)
     flip[0:512] = dh_mid[...].T
 
     def spatial_term(weight, patch, first_tap, last_tap, tensor):
@@ -1782,9 +1781,8 @@
         HAT_B1,
         2,
         4,
-        [spatial_term(w_b2, saved[PATCH_B], 0, 3, 5), spatial_term(w_b2, saved[PATCH_B], 3, 6, 5)],
-    )
-    pump()
+        [spatial_term(w_b2, saved[PATCH_B], 0, 3, 5), pump, spatial_term(w_b2, saved[PATCH_B], 3, 6, 5), pump],
+    )
     spatial_term(w_b2, saved[PATCH_B], 6, 9, 5)()
     pump()
     loading(PATCH_A).start()
@@ -1794,7 +1792,8 @@
         dz[:, at] = dz[:, at] + dot(dh_mid[...], w_b1[:, :, 0, :, at].reshape(512, 256))
         return carry
 
-    paced(0, 8, residual, 2, pump)
+    lax.fori_loop(0, 8, residual, 0)
+    pump()
     for name in order[4:]:
         loading(name).wait()
 
@@ -1806,7 +1805,7 @@
         return [(value, saved[HAT_A3][:, at].astype(jnp.float32))]
 
     total = sums[SUM_J]
-    put_sums(plan, join_pairs, mask, total.pay, 0, 2048, pump)
+    put_sums(plan, join_pairs, mask, total.pay, 0, 2048)
     put_sums(
         plan, lambda j: [(dz[:, columns(j)], saved[HAT_AS][:, columns(j)].astype(jnp.float32))], mask, total.pay, 16, 2048
     )
@@ -1824,6 +1823,7 @@
             lax.fori_loop(2 * part, 2 * part + 2, body, 0)
             if part == 3:
                 reduce.enable(4)
+            pump()
 
         return work
 
@@ -1843,6 +1843,7 @@
     def third_term_a():
         expand_term(flip[0:512, :], dh_a, w_a3, 0, 8)
         reduce.enable(2)
+        pump()
 
     def shortcut():
         even = dz.at[:, 0:1024]
@@ -1863,7 +1864,7 @@
 
         lax.fori_loop(0, 8, keep, 0)
 
-    mid_norm(SUM_A2, HAT_A2, 1, 2, [third_term_a, shortcut])
+    mid_norm(SUM_A2, HAT_A2, 1, 2, [third_term_a, shortcut, pump])
 
     loading(PATCH_A).wait()
     flip[...] = x[0].T
@@ -1908,8 +1909,10 @@
     flip[0:512] = dh_mid[...].T
     stages = total.stages()
     spatial_term(w_a2, saved[PATCH_A], 0, 3, 1)()
+    pump()
     stages[0]()
     spatial_term(w_a2, saved[PATCH_A], 3, 6, 1)()
+    pump()
     stages[1]()
     pump()
     spatial_term(w_a2, saved[PATCH_A], 6, 9, 1)()

time: 466 us -> 440 us (0.944)
  Pallas kernels: 420 us -> 395 us
    pallas_call x1, Pallas kernels: 223 us -> 209 us  [run_backward(): pl.pallas_call(functools.partial(backward_kernel, plan, depth), out_shape...]
    pallas_call x1, Pallas kernels: 190 us -> 178 us  [run_forward(): pl.pallas_call(functools.partial(forward_kernel, plan, depth), out_shape=...]
where the time goes in v2:
time: 440 us; the launch traced here: 432 us
  Pallas kernels  395 us (90%)
  local copies, waits for them, and re-layouts  28.3 us (6%)
  other arithmetic  6.79 us (2%)
    pallas_call x1, Pallas kernels, run_backward(): pl.pallas_call(functools.partial(backward_kernel, plan, depth), out_shape...  209 us
    pallas_call x1, Pallas kernels, run_forward(): pl.pallas_call(functools.partial(forward_kernel, plan, depth), out_shape=...  178 us

profile of v2, /device:TPU:0, one launch (start us, length us, event | category | flops | bytes accessed | tf_op | source)
XLA Modules:
  0.0 431.7 jit_solution(18229735881614638506)
XLA Ops:
  0.7 0.7 convert_element_type.23
  1.3 0.5 pad.37.refs_3_
  1.8 0.7 maximum_convert_fusion
  2.6 1.3 fusion.17.refs_5_
  3.9 0.1 dynamic_update_slice.3.refs_4_
  4.0 0.0 copy-start.2
  4.0 1.1 reshape.169
  5.1 0.0 copy-done.2
  5.1 0.0 copy-start.1
  5.2 1.2 reshape.170
  6.4 2.1 reshape.171
  8.5 1.2 fusion.11.refs_2_
  9.7 0.0 copy-done.1
  9.7 0.0 copy-start
  9.7 0.8 copy.77
  10.6 0.3 reshape.158
  10.9 0.2 copy.64
  11.2 0.0 copy-done
  11.2 0.3 copy.76
  11.5 1.1 reshape.156
  12.6 2.2 copy.75
  14.8 0.5 reshape.160
  15.4 2.9 fusion.5.refs_0_
  18.2 178.3 %shard_map.438 = (bf16[100,2048]{1,0:T(8,128)(2,1)}, bf16[98,2048]{1,0:T(8,128)(2,1)}, bf16[162,2048]{1,0:T(8,128)(2,1)}, f32[384,128]{1,0:T(8,128)}, f32[4,8,51...) custom-call(bf16[4,384,1024]{2,1,0:T(8,128)(2,1)} %fusion.5.refs_0_,, ...), custom_call_target="tpu_custom_call" | custom-call | tf_op jit(solution)/shard_map/pallas_call | solution.py:1591
  196.5 1.9 reshape.166
  198.4 2.0 reshape.167
  200.5 2.6 reshape.168
  203.1 209.1 %shard_map.439 = (bf16[4,384,1024]{2,1,0:T(8,128)(2,1)}, f32[4,8,512]{2,1,0:T(8,128)}, f32[8,2048]{1,0:T(8,128)}, f32[8,4096]{1,0:T(8,128)}, f32[8,128]{1,0:T(8,...) custom-call(bf16[4,384,1024]{2,1,0:T(8,128)(2,1)} %fusion.5.refs_0_,, ...), custom_call_target="tpu_custom_call" | custom-call | tf_op jit(solution)/shard_map/pallas_call | solution.py:1994
  412.3 1.2 slice.10
  413.5 0.6 reshape.188
  414.0 1.6 copy.68
  415.6 1.2 slice.9
  416.9 1.4 slice.11
  418.3 1.0 reshape.176
  419.3 0.4 reshape.172
  419.6 1.4 copy.66
  421.0 2.3 copy.69
  423.3 7.9 %shard_map.440 = (f32[1,64,1024]{2,1,0:T(8,128)}, f32[1,64,1024]{2,1,0:T(8,128)}, f32[9,64,512]{2,1,0:T(8,128)}, f32[9,64,512]{2,1,0:T(8,128)}, f32[2,256,256]{2...) custom-call(f32[8,128]{1,0:T(8,128)} %get-tuple-element.121.squares,, ...), custom_call_target="tpu_custom_call" | custom-call | tf_op jit(solution)/shard_map/pallas_call | solution.py:2096
  (1 shorter events, 0.0 us)
Async XLA Ops:
  4.0 1.1 copy-start.2
  5.1 4.6 %copy-start.1 = (bf16[2,14,14,1024]{3,0,2,1:T(2,128)(2,1)S(1)}, bf16[2,14,14,1024]{3,0,2,1:T(2,128)(2,1)}, u32[]{:S(2)}) copy-start(bf16[2,14,14,1024]{3,0,2,1:T(2,128)(2,1)} %param.24) | copy-start | bytes 2408452
  9.7 1.4 copy-start
